TPU v7x, 128 devices: a whole 4x4x4 slice. The times are simulated.
128 devices in a mesh: row: 16 (over y_lo, z, core), col: 8 (over x, y_hi).
Axes of the slice: x: 4, y: 4 (y_hi: 2, y_lo: 2; y = y_hi * 2 + y_lo), z: 4, core: 2. Of those that a mesh axis runs over, the one named last changes fastest.
Arguments:
- front: float32 [8, 2048, 16, 1024], P(None, 'row', None, 'col')
- child_blocks: float32 [2, 4, 2048, 8, 1024], P(None, None, 'row', None, 'col')
- child_map: int32 [2, 64], replicated, may hold values from 0 to 127, as said below
Outputs:
- factored: float32 [8, 2048, 16, 1024], P(None, 'row', None, 'col')
Inputs may be any that keep to these rules, and one draw needn't show every extreme that they name: Each child's entries are distinct. For each child h and each k below 4, (child_map[h, t] - t) mod 16 is the same for all t with t // 16 = k. Of the tiles t with one value of t mod 16, over both children, at most 1 share one value of child_map mod 16; of one child's tiles t with one value of t mod 8, at most 2 share one value of child_map mod 8; both bounds are reached in every draw.
All inputs are finite; a program needn't handle non-finite values.
Results may differ from a plain program's by a relative error of at most 0.0001.
Values sent between devices are 32-bit elements; how exact they have to be, the bound alone decides.
No kernel may reach another device: no remote copies, remote signals or barrier semaphores. Data moves between devices by JAX's collectives and lax.ppermute only.
A program may use at most 192 MiB of HBM per device.

v0:
```python
import jax
import jax.numpy as jnp
from jax import lax
from jax.sharding import PartitionSpec as P

PANEL_WIDTH = 512
PANELS = 2


HIGHEST_PRECISION = lax.Precision.HIGHEST


def rank_earlier(labels):
    length = labels.shape[-1]
    same = labels[..., :, None] == labels[..., None, :]
    earlier = jnp.arange(length)[None, :] < jnp.arange(length)[:, None]
    return jnp.sum(same & earlier, axis=-1)


def column_tables(child_map, column, col_count, count, slots):
    tiles = column + col_count * jnp.arange(count)
    target = child_map[:, tiles]
    owner = target % col_count
    local = target // col_count
    ranked = rank_earlier(owner)
    return (owner, ranked, local, owner * slots + ranked)


def mixed(form, left, right):
    return jnp.einsum(
        form, left, right, precision=HIGHEST_PRECISION, preferred_element_type=jnp.float32
    )


def shards(front, child_blocks, child_map):
    row_count = lax.axis_size("row")
    col_count = lax.axis_size("col")
    row_place = lax.axis_index("row")
    col_place = lax.axis_index("col")
    row_tiles, square, col_tiles, _ = front.shape
    child_rows = child_blocks.shape[1]
    child_cols = child_blocks.shape[3]
    row_total = 2 * child_rows
    row_slots = max(1, row_total // row_count)
    col_slots = row_count // col_count * max(1, child_rows // col_count)
    child_of = jnp.arange(row_total) // child_rows
    level_of = jnp.arange(row_total) % child_rows
    shifts = (child_map[:, row_count * jnp.arange(child_rows)] % row_count).reshape(-1)
    row_rank = rank_earlier(shifts)
    send_slot = (row_place + shifts) % row_count * row_slots + row_rank
    source_row = (row_place - shifts) % row_count
    take_slot = source_row * row_slots + row_rank
    slot_range = jnp.arange(row_count * row_slots)
    send_hot = (send_slot[:, None] == slot_range).astype(jnp.float32)
    take_hot = (take_slot[:, None] == slot_range).astype(jnp.float32)
    parent_row = child_map[child_of, source_row + row_count * level_of] // row_count
    row_hot = (parent_row[:, None] == jnp.arange(row_tiles)).astype(jnp.float32)
    _, _, _, col_position = column_tables(child_map, col_place, col_count, child_cols, col_slots)
    place_hot = (col_position[child_of][:, :, None] == jnp.arange(col_count * col_slots)).astype(
        jnp.float32
    )
    all_owner, all_rank, all_local, _ = column_tables(
        child_map, jnp.arange(col_count)[:, None], col_count, child_cols, col_slots
    )
    matched = (all_owner == col_place)[..., None] & (all_rank[..., None] == jnp.arange(col_slots))
    slot_local = jnp.sum(jnp.where(matched, all_local[..., None], 0), axis=2).reshape(
        2, col_count * col_slots
    )
    slot_valid = jnp.any(matched, axis=2).reshape(2, col_count * col_slots)
    child_tiles = child_blocks.reshape(row_total, square, child_cols, square)
    outgoing = mixed("jamb,jd->damb", child_tiles, send_hot)
    incoming = lax.all_to_all(outgoing, "row", split_axis=0, concat_axis=0, tiled=True)
    arrived = mixed("damb,jd->jamb", incoming, take_hot)
    spread = mixed("jamb,jmp->japb", arrived, place_hot)
    landed = lax.all_to_all(spread, "col", split_axis=2, concat_axis=2, tiled=True)
    col_hot = (slot_valid[..., None] & (slot_local[..., None] == jnp.arange(col_tiles))).astype(
        jnp.float32
    )
    placed = mixed("japb,jpn->janb", landed, col_hot[child_of])
    matrix = front + mixed("janb,jk->kanb", placed, row_hot)
    rows_global = square * (row_place + row_count * jnp.arange(row_tiles))[:, None] + jnp.arange(
        square
    )
    cols_global = square * (col_place + col_count * jnp.arange(col_tiles))[:, None] + jnp.arange(
        square
    )
    rows_flat = rows_global.reshape(-1)
    cols_flat = cols_global.reshape(-1)
    panel_tiles = PANEL_WIDTH // square
    for panel in range(PANELS):
        start = panel * PANEL_WIDTH
        stop = start + PANEL_WIDTH
        pieces = []
        for position in range(panel_tiles):
            serial = panel * panel_tiles + position
            pieces.append(
                jnp.where(
                    col_place == serial % col_count,
                    matrix[:, :, serial // col_count, :],
                    jnp.float32(0.0),
                )
            )
        stacked = jnp.stack(pieces, axis=2).reshape(row_tiles, square, PANEL_WIDTH)
        panel_rows = lax.psum(stacked, "col").reshape(row_tiles * square, PANEL_WIDTH)
        block_pieces = []
        for position in range(panel_tiles):
            serial = panel * panel_tiles + position
            block_pieces.append(
                jnp.where(
                    row_place == serial % row_count, matrix[serial // row_count], jnp.float32(0.0)
                )
            )
        block = lax.psum(jnp.stack(block_pieces), "row").reshape(PANEL_WIDTH, col_tiles, square)
        diag_pieces = []
        for position in range(panel_tiles):
            serial = panel * panel_tiles + position
            diag_pieces.append(
                jnp.where(
                    col_place == serial % col_count,
                    block[:, serial // col_count, :],
                    jnp.float32(0.0),
                )
            )
        diagonal = lax.psum(jnp.stack(diag_pieces, axis=1), "col").reshape(PANEL_WIDTH, PANEL_WIDTH)
        lower = jnp.linalg.cholesky(diagonal)
        factor = jax.scipy.linalg.solve_triangular(lower, panel_rows.T, lower=True).T
        factor = jnp.where(rows_flat[:, None] >= start, factor, jnp.float32(0.0))
        col_factor = jax.scipy.linalg.solve_triangular(
            lower, block.reshape(PANEL_WIDTH, col_tiles * square), lower=True
        ).T
        col_factor = jnp.where(cols_flat[:, None] >= start, col_factor, jnp.float32(0.0))
        row_trail = rows_flat >= stop
        col_trail = cols_flat >= stop
        product = jnp.dot(
            factor, col_factor.T, precision=HIGHEST_PRECISION, preferred_element_type=jnp.float32
        )
        keep = row_trail[:, None] & col_trail[None, 0 * square : col_tiles * square]
        matrix = matrix - jnp.where(keep, product, jnp.float32(0.0)).reshape(
            row_tiles, square, col_tiles - 0, square
        )
        shaped_factor = factor.reshape(row_tiles, square, PANEL_WIDTH)
        row_mask = (rows_global >= start)[:, :, None]
        for position in range(panel_tiles):
            serial = panel * panel_tiles + position
            local_col = serial // col_count
            owned = col_place == serial % col_count
            current = matrix[:, :, local_col, :]
            update = shaped_factor[:, :, position * square : (position + 1) * square]
            matrix = matrix.at[:, :, local_col, :].set(jnp.where(owned & row_mask, update, current))
    return matrix


def solution(mesh):
    in_specs = (P(None, "row", None, "col"), P(None, None, "row", None, "col"), P())
    out_specs = P(None, "row", None, "col")
    return jax.shard_map(shards, mesh=mesh, in_specs=in_specs, out_specs=out_specs, check_vma=False)
```

profile of v0, /device:TPU:1, one launch (start us, length us, event | category | flops | bytes accessed | tf_op | source)
XLA Modules:
  0.0 1338.9 jit_solution(10257584719433476356)
XLA Ops:
  8.3 7.9 fusion.22
  22.2 8.2 all-to-all-start
  32.1 120.4 %all-to-all-done = f32[16,128,8,128]{3,2,1,0:T(8,128)} async-done(((f32[16,128,8,128]{3,2,1,0:T(8,128)}), f32[16,128,8,128]{3,2,1,0:T(8,128)}, u32[]{:S(2)}, u32[]{:S(2)}) %all-to-all-start) | async-done | bytes 8388640 | tf_op jit(solution)/shard_map/all_to_all | solution.py:72
  152.6 10.9 fusion.4
  183.5 111.3 %all-to-all-done.1 = f32[8,128,16,128]{3,1,0,2:T(8,128)} async-done(((f32[8,128,16,128]{3,1,0,2:T(8,128)}), f32[8,128,16,128]{3,1,0,2:T(8,128)}, u32[]{:S(2)}, u32[]{:S(2)}) %all-to-all-start.1) | async-done | bytes 8388640 | tf_op jit(solution)/shard_map/all_to_all | solution.py:75
  294.8 11.7 fusion.26
  306.5 15.4 %copy_add_fusion = f32[8,128,16,128]{3,0,2,1:T(8,128)S(1)} fusion(f32[8,128,16,128]{3,2,1,0:T(8,128)} %param.24, f32[8,128,16,128]{3,2,1,0:T(8,128)S(1)} %fusion.26, s32[8]{0:T(128)S(1)} %and_select_fusion.3), kind=kOutput, calls=%fused_computation.12 | convolution fusion | flops 203423808 | bytes 25165856 | tf_op jit(solution)/shard_map/janb,jk->kanb/dot_general | solution.py:30
  340.3 129.2 %all-reduce.8.cloned.1.call-done = f32[4,128,16,128]{3,0,2,1:T(4,128)} async-done(((f32[4,128,16,128]{3,0,2,1:T(4,128)}), f32[4,128,16,128]{3,0,2,1:T(4,128)}) %all-reduce.8.cloned.1.call-update) | async-done | bytes 4194320 | tf_op jit(solution)/shard_map/psum | solution.py:113
  484.0 140.5 %all-reduce.14.cloned.1.call-done = (f32[512,512]{0,1:T(8,128)}, f32[512,1024]{1,0:T(8,128)}) async-done(((f32[512,512]{0,1:T(8,128)}, f32[512,1024]{1,0:T(8,128)}), (f32[512,512]{0,1:T(8,128)}, f32[512,1024]{1,0:T(8,128)})) %all-reduce.14.cloned.1.call-update) | async-done | bytes 3145744 | tf_op jit(solution)/shard_map/psum | solution.py:124
  627.5 11.7 cholesky.286
  639.4 9.8 custom-call.33
  649.8 11.9 cholesky.305
  663.1 9.8 custom-call.34
  673.6 11.7 cholesky.326
  686.1 9.8 custom-call.35
  696.5 12.1 cholesky.343
  719.7 39.3 %custom-call.36 = f32[4,128,128]{1,2,0:T(8,128)S(1)} custom-call(f32[4,128,128]{2,1,0:T(8,128)S(1)} %get-tuple-element.132), custom_call_target="InvertDiagBlocksLowerTriangular" | custom-call | tf_op jit(solution)/shard_map/jit(_solve_triangular)/triangular_solve | solution.py:126
  783.6 15.2 %select_bitcast_fusion.1 = f32[128,8,16,128]{3,1,2,0:T(8,128)S(1)} fusion(pred[2048]{0:T(1024)(128)(4,1)S(1)} %get-tuple-element.234, pred[1024]{0:T(1024)(128)(4,1)S(1)} %get-tuple-element.231, f32[128,2048]{1,0:T(8,128)S(1)} %fusion.139, f32[128,2048]{1,0:T(8,128)S(1)} %fusion.137, f32[128,2048]{1,0:T(8,128)S(1)} %fusion.135, ...), kind=kOutput, calls=%fused_computation.20 | convolution fusion | flops 12895387648 | bytes 14686208 | tf_op jit(solution)/shard_map/dot_general | solution.py:134
  804.4 14.3 %copy_subtract_fusion.1 = f32[8,128,16,128]{3,0,2,1:T(8,128)} fusion(f32[8,128,16,128]{3,0,2,1:T(8,128)} %copy-done.1, f32[8,128,16,128]{3,2,1,0:T(8,128)} %bitcast.312), kind=kLoop, calls=%fused_computation.11 | loop fusion | flops 2097152 | bytes 25165824 | tf_op jit(solution)/shard_map/sub | solution.py:138
  841.7 125.8 %all-reduce.10.cloned.1.call-done = f32[4,128,16,128]{3,0,2,1:T(4,128)} async-done(((f32[4,128,16,128]{3,0,2,1:T(4,128)}), f32[4,128,16,128]{3,0,2,1:T(4,128)}) %all-reduce.10.cloned.1.call-update) | async-done | bytes 4194320 | tf_op jit(solution)/shard_map/psum | solution.py:113
  981.5 141.8 %all-reduce.12.cloned.1.call-done = (f32[512,512]{0,1:T(8,128)}, f32[512,1024]{1,0:T(8,128)}) async-done(((f32[512,512]{0,1:T(8,128)}, f32[512,1024]{1,0:T(8,128)}), (f32[512,512]{0,1:T(8,128)}, f32[512,1024]{1,0:T(8,128)})) %all-reduce.12.cloned.1.call-update) | async-done | bytes 3145744 | tf_op jit(solution)/shard_map/psum | solution.py:124
  1126.3 11.7 cholesky.358
  1138.2 9.8 custom-call.38
  1149.1 11.7 cholesky.377
  1162.2 9.8 custom-call.39
  1172.7 11.7 cholesky.398
  1185.1 10.0 custom-call.40
  1195.7 11.7 cholesky.415
  1218.6 39.3 %custom-call.41 = f32[4,128,128]{1,2,0:T(8,128)S(1)} custom-call(f32[4,128,128]{2,1,0:T(8,128)S(1)} %get-tuple-element.134), custom_call_target="InvertDiagBlocksLowerTriangular" | custom-call | tf_op jit(solution)/shard_map/jit(_solve_triangular)/triangular_solve | solution.py:126
  1282.7 15.2 %select_bitcast_fusion = f32[128,8,16,128]{3,1,2,0:T(8,128)S(1)} fusion(pred[2048]{0:T(1024)(128)(4,1)S(1)} %get-tuple-element.232, pred[1024]{0:T(1024)(128)(4,1)S(1)} %get-tuple-element.222, f32[128,2048]{1,0:T(8,128)S(1)} %fusion.145, f32[128,2048]{1,0:T(8,128)S(1)} %fusion.143, f32[128,2048]{1,0:T(8,128)S(1)} %fusion.141, f32[128,2048]{1,0:T(8,128)S(1)} %fusion.80, ...), kind=kOutput, calls=%fused_computation.19 | convolution fusion | flops 12895387648 | bytes 14686208 | tf_op jit(solution)/shard_map/dot_general | solution.py:134
  1303.3 14.1 %copy_subtract_fusion = f32[8,128,16,128]{3,0,2,1:T(8,128)} fusion(f32[8,128,16,128]{3,0,2,1:T(8,128)} %bitcast_dynamic-update-slice_fusion.8, f32[8,128,16,128]{3,2,1,0:T(8,128)} %bitcast.313), kind=kLoop, calls=%fused_computation.10 | loop fusion | flops 2097152 | bytes 25165824 | tf_op jit(solution)/shard_map/sub | solution.py:138
  1323.7 8.4 copy.299
  (241 shorter events, 212.9 us)
Async XLA Ops:
  22.2 130.4 %all-to-all-start = ((f32[16,128,8,128]{3,2,1,0:T(8,128)}), f32[16,128,8,128]{3,2,1,0:T(8,128)}, u32[]{:S(2)}, u32[]{:S(2)}) async-start(f32[16,128,8,128]{3,2,1,0:T(8,128)} %copy.253), calls=%async_computation | async-start | bytes 16777216 | tf_op jit(solution)/shard_map/all_to_all | solution.py:72
  173.3 9.5 copy-start
  173.3 121.5 %all-to-all-start.1 = ((f32[8,128,16,128]{3,1,0,2:T(8,128)}), f32[8,128,16,128]{3,1,0,2:T(8,128)}, u32[]{:S(2)}, u32[]{:S(2)}) async-start(f32[8,128,16,128]{3,1,0,2:T(8,128)} %copy.256), calls=%async_computation.1 | async-start | bytes 16777216 | tf_op jit(solution)/shard_map/all_to_all | solution.py:75
  179.8 289.7 %all-reduce.8.cloned.1.call-start = ((), (), s32[]{:S(2)}) async-start(), calls=%async_computation.2 | async-start | bytes 8388608 | tf_op jit(solution)/shard_map/psum | solution.py:113
  322.0 3.4 copy-start.1
  333.5 290.9 %all-reduce.14.cloned.1.call-start = ((), (), s32[]{:S(2)}) async-start(), calls=%async_computation.5 | async-start | bytes 6291456 | tf_op jit(solution)/shard_map/psum | solution.py:124
  472.0 2.0 copy-start.2
  476.9 490.5 %all-reduce.10.cloned.1.call-start = ((), (), s32[]{:S(2)}) async-start(), calls=%async_computation.3 | async-start | bytes 8388608 | tf_op jit(solution)/shard_map/psum | solution.py:113
  719.7 45.9 %copy-start.11 = (f32[512,512]{1,0:T(8,128)}, f32[512,512]{1,0:T(8,128)S(1)}, u32[]{:S(2)}) copy-start(f32[512,512]{1,0:T(8,128)S(1)} %get-tuple-element.353) | copy-start | bytes 3145732
  759.1 4.1 copy-start.16
  764.5 1.8 copy-start.8
  766.3 0.8 copy-start.14
  769.4 2.9 copy-start.5
  779.5 4.1 copy-start.9
  779.5 4.1 copy-start.15
  836.0 287.3 %all-reduce.12.cloned.1.call-start = ((), (), s32[]{:S(2)}) async-start(), calls=%async_computation.4 | async-start | bytes 6291456 | tf_op jit(solution)/shard_map/psum | solution.py:124
  970.0 2.0 copy-start.3
  1218.6 45.9 %copy-start.10 = (f32[512,512]{1,0:T(8,128)}, f32[512,512]{1,0:T(8,128)S(1)}, u32[]{:S(2)}) copy-start(f32[512,512]{1,0:T(8,128)S(1)} %get-tuple-element.352) | copy-start | bytes 3145732
  1257.9 4.1 copy-start.17
  1263.4 1.8 copy-start.6
  1265.2 0.8 copy-start.12
  1268.5 2.9 copy-start.4
  1278.5 4.1 copy-start.7
  1278.5 4.1 copy-start.13
Sparse Core Ops, SparseCore 0:
  333.6 135.7 all-reduce.7
  477.1 147.3 all-reduce.13
  836.1 131.3 all-reduce.9
  975.1 148.1 all-reduce.11
where the time goes:
time: 1350 us; the launch traced here: 1340 us
  waiting for transfers between devices  769 us (57%)
  other arithmetic  304 us (23%)
  matrix products  121 us (9%)
  local copies, waits for them, and re-layouts  110 us (8%)
  between operations  19.4 us (1%)
  starting transfers between devices  15.4 us (1%)
    psum x2, waiting for transfers between devices, shards(): lax.psum(jnp.stack(diag_pieces, axis=1), 'col')  282 us
    psum x2, waiting for transfers between devices, shards(): lax.psum(jnp.stack(block_pieces), 'row')  255 us
    another operation x30, other arithmetic, shards(): lower = jnp.linalg.cholesky(diagonal)  159 us
    all_to_all x1, waiting for transfers between devices, shards(): lax.all_to_all(outgoing, 'row', split_axis=0, concat_axis=0, tiled=True)  120 us
    all_to_all x1, waiting for transfers between devices, shards(): lax.all_to_all(spread, 'col', split_axis=2, concat_axis=2, tiled=True)  111 us
    another operation x5, other arithmetic, shards(): jax.scipy.linalg.solve_triangular(lower, panel_rows.T, lower=True)  78.9 us
    dot_general x5, matrix products, mixed(): jnp.einsum(form, left, right, precision=HIGHEST_PRECISION, preferred_elem...  49.8 us
    unnamed x43, local copies, waits for them, and re-layouts  41.6 us
  transfers between devices with their start and end apart: 6, of which 6 were waited for; matrix products, arithmetic and copies ran while one was open for 2% of the time, Pallas kernels for 0%

commit v1 on v0

v1 whole, which is shorter than its diff:
```python
import functools

import jax
import jax.numpy as jnp
from jax import lax
from jax.experimental import pallas as pl
from jax.experimental.pallas import tpu as pltpu
from jax.sharding import PartitionSpec as P

T = 128
W = 1024
F32 = jnp.float32
BF16 = jnp.bfloat16
HIGHEST = lax.Precision.HIGHEST
ROW_AT = 128
COL_AT = 129
VMEM = 58 * 1024 * 1024


def params(**kw):
    return pltpu.CompilerParams(vmem_limit_bytes=VMEM, **kw)


def shift(meta, h, k):
    return meta[h * 64 + 16 * k] & 15


def source_row(meta, h, ka):
    return (meta[ROW_AT] - shift(meta, h, ka)) & 15


def local_row(meta, h, ka):
    return meta[h * 64 + source_row(meta, h, ka) + 16 * ka] >> 4


def level_of(meta, h, a):
    ka = jnp.int32(0)
    found = jnp.int32(0)
    for k in range(4):
        hit = local_row(meta, h, k) == a
        ka = jnp.where(hit, k, ka)
        found = jnp.where(hit, 1, found)
    return ka, found


def dest_col(meta, h, kb):
    return (meta[COL_AT] + shift(meta, h, kb)) & 7


def source_col(meta, h, kb):
    return (meta[COL_AT] - shift(meta, h, kb)) & 7


def local_col(meta, h, kb, i):
    return meta[h * 64 + source_col(meta, h, kb) + 8 * (2 * kb + i)] >> 3


def split(x):
    hi = x.astype(BF16)
    return hi, (x - hi.astype(F32)).astype(BF16)


def dot(a, b, dims=((1,), (0,)), precision=None):
    return lax.dot_general(a, b, (dims, ((), ())), precision=precision, preferred_element_type=F32)


NT = ((1,), (1,))


def dot3(a, b, dims=((1,), (0,))):
    return dot(a[0], b[0], dims) + (dot(a[0], b[1], dims) + dot(a[1], b[0], dims))


def pack_rows_kernel(meta, child_ref, out_ref):
    flat = child_ref.reshape(T * 8, T)
    for j in range(8):
        out_ref[0, j] = flat[pl.ds(j, T, stride=8), :]


def pack_rows(meta, child):
    return pl.pallas_call(
        pack_rows_kernel,
        grid_spec=pltpu.PrefetchScalarGridSpec(
            num_scalar_prefetch=1,
            grid=(2, 4),
            in_specs=[pl.BlockSpec((None, None, T, 8, T), lambda h, k, m: (h, k, 0, 0, 0))],
            out_specs=pl.BlockSpec(
                (1, 8, T, T), lambda h, k, m: ((m[ROW_AT] + shift(m, h, k)) & 15, 0, 0, 0)
            ),
        ),
        out_shape=jax.ShapeDtypeStruct((16, 8, T, T), F32),
        compiler_params=params(),
        name="pack_rows",
    )(meta, child)


def pack_cols_kernel(levels, meta, arrived, out, sems):
    copies = []
    for h in range(2):
        for lev in range(levels):
            if levels == 1:
                ka, _ = level_of(meta, h, 0)
            else:
                ka = lev
            src = source_row(meta, h, ka)
            for kb in range(4):
                copies.append(
                    pltpu.make_async_copy(
                        arrived.at[src, pl.ds(2 * kb, 2)],
                        out.at[dest_col(meta, h, kb), h, lev],
                        sems.at[len(copies)],
                    )
                )
    for c in copies:
        c.start()
    for c in copies:
        c.wait()


def pack_cols(meta, arrived, levels):
    return pl.pallas_call(
        functools.partial(pack_cols_kernel, levels),
        in_specs=[pl.BlockSpec(memory_space=pltpu.SMEM), pl.BlockSpec(memory_space=pl.ANY)],
        out_specs=pl.BlockSpec(memory_space=pl.ANY),
        out_shape=jax.ShapeDtypeStruct((8, 2, levels, 2, T, T), F32),
        scratch_shapes=[pltpu.SemaphoreType.DMA((8 * levels,))],
        name=f"pack_cols_{levels}",
    )(meta, arrived)


def first_row_kernel(meta, front_ref, got_ref, out_ref):
    flat = front_ref.reshape(T * 16, T)
    for lc in range(16):
        out_ref[(lc % 2) * 8 + lc // 2] = flat[pl.ds(lc, T, stride=16), :]
    for h in range(2):
        _, found = level_of(meta, h, 0)

        @pl.when(found == 1)
        def _():
            for kb in range(4):
                src = source_col(meta, h, kb)
                for i in range(2):
                    lc = local_col(meta, h, kb, i)
                    at = (lc & 1) * 8 + (lc >> 1)
                    out_ref[at] = out_ref[at] + got_ref[src, h, 0, i]


def first_row(meta, front, got):
    return pl.pallas_call(
        first_row_kernel,
        grid_spec=pltpu.PrefetchScalarGridSpec(
            num_scalar_prefetch=1,
            grid=(1,),
            in_specs=[
                pl.BlockSpec((None, T, 16, T), lambda i, m: (0, 0, 0, 0)),
                pl.BlockSpec((8, 2, 1, 2, T, T), lambda i, m: (0, 0, 0, 0, 0, 0)),
            ],
            out_specs=pl.BlockSpec((16, T, T), lambda i, m: (0, 0, 0)),
        ),
        out_shape=jax.ShapeDtypeStruct((16, T, T), F32),
        compiler_params=params(),
        name="first_row",
    )(meta, front, got)


def invert_kernel(pieces, hi_ref, lo_ref, a_ref, t_ref, l_ref):
    for q in range(8):
        for c in range(8):
            for half in range(2):
                a_ref[q * T + half * 64 : q * T + half * 64 + 64, c * T : (c + 1) * T] = pieces[
                    q + 8 * half, c
                ]
    t_ref[...] = jnp.zeros_like(t_ref)
    sub = lax.broadcasted_iota(jnp.int32, (8, T), 0)
    lane = lax.broadcasted_iota(jnp.int32, (8, T), 1)

    def step(k, _):
        at = pl.multiple_of(k * T, T)
        s = [a_ref[pl.ds(at + 8 * b, 8), pl.ds(at, T)] for b in range(16)]
        t = [jnp.where(lane == sub + 8 * b, F32(1), F32(0)) for b in range(16)]
        for j in range(T):
            b0, i0 = divmod(j, 8)
            pivot = s[b0][i0 : i0 + 1, j : j + 1]
            r = lax.rsqrt(pivot)
            r = r * (1.5 - 0.5 * pivot * r * r)
            u = jnp.broadcast_to(s[b0][i0 : i0 + 1, :], (8, T)) * r
            w = jnp.broadcast_to(t[b0][i0 : i0 + 1, :], (8, T)) * r
            for b in range(b0, 16):
                v = jnp.broadcast_to(s[b][:, j : j + 1], (8, T)) * r
                if b == b0:
                    v = jnp.where(sub > i0, v, F32(0))
                    t[b] = jnp.where(sub == i0, w, t[b] - v * w)
                else:
                    t[b] = t[b] - v * w
                s[b] = s[b] - v * u
        kinv = jnp.concatenate(t, axis=0)
        for kk in range(8):

            @pl.when(k == kk)
            def _():
                lo, hi = kk * T, (kk + 1) * T
                if kk:
                    t_ref[lo:hi, :lo] = dot(kinv, t_ref[lo:hi, :lo], precision=HIGHEST)
                t_ref[lo:hi, lo:hi] = kinv
                if kk < 7:
                    col = dot(a_ref[hi:, lo:hi], kinv, NT, precision=HIGHEST)
                    l_ref[hi:, :] = col
                    for n0 in range(hi, W, T):
                        a_ref[n0:, n0 : n0 + T] = a_ref[n0:, n0 : n0 + T] - dot(
                            l_ref[n0:, :], l_ref[n0 : n0 + T, :], NT, precision=HIGHEST
                        )
                    t_ref[hi:, :hi] = t_ref[hi:, :hi] - dot(
                        l_ref[hi:, :], t_ref[lo:hi, :hi], precision=HIGHEST
                    )

        return 0

    lax.fori_loop(0, 8, step, 0)
    hi_ref[...], lo_ref[...] = split(t_ref[...])


def invert(pieces):
    return pl.pallas_call(
        invert_kernel,
        out_shape=[jax.ShapeDtypeStruct((W, W), BF16)] * 2,
        scratch_shapes=[
            pltpu.VMEM((W, W), F32),
            pltpu.VMEM((W, W), F32),
            pltpu.VMEM((W, T), F32),
        ],
        compiler_params=params(),
        cost_estimate=pl.CostEstimate(flops=80_000_000_000, bytes_accessed=8 << 20, transcendentals=0),
        name="invert",
    )(pieces)


B = 256


def solve_cols_kernel(ihi, ilo, x_ref, ohi, olo):
    x = jnp.concatenate(
        [jnp.concatenate([x_ref[q, 0], x_ref[q, 1]], axis=1) for q in range(8)], axis=0
    )
    xs = split(x)
    for k in range(W // B):
        n = (k + 1) * B
        rows = slice(k * B, n)
        y = dot3((ihi[rows, :n], ilo[rows, :n]), (xs[0][:n], xs[1][:n]))
        ohi[rows, :], olo[rows, :] = split(y)


def solve_cols(inverse, x):
    whole = pl.BlockSpec((W, W), lambda i: (0, 0))
    out = pl.BlockSpec((W, B), lambda i: (0, i))
    return pl.pallas_call(
        solve_cols_kernel,
        grid=(8,),
        in_specs=[
            whole,
            whole,
            pl.BlockSpec((None, 8, 2, T, T), lambda i: (i // 4, 0, i % 4, 0, 0)),
        ],
        out_specs=[out, out],
        out_shape=[jax.ShapeDtypeStruct((W, 2048), BF16)] * 2,
        compiler_params=params(),
        name="solve_cols",
    )(*inverse, x)


def solve_rows_kernel(meta, ihi, ilo, x_ref, ohi, olo, pan, y_ref):
    x = jnp.concatenate(
        [jnp.concatenate([x_ref[q, a] for q in range(8)], axis=1) for a in range(2)], axis=0
    )
    xs = split(x)
    for k in range(W // B):
        n = (k + 1) * B
        rows = slice(k * B, n)
        y_ref[:, rows] = dot3((xs[0][:, :n], xs[1][:, :n]), (ihi[rows, :n], ilo[rows, :n]), NT)
    at = pl.multiple_of(meta[COL_AT] * T, T)
    for a in range(2):
        pan[a] = y_ref[a * T : (a + 1) * T, pl.ds(at, T)]
    row = meta[ROW_AT]
    limit = jnp.where(row < 4, 0, jnp.where(row < 8, 512, W))
    limit = jnp.where(pl.program_id(0) == 0, limit, W)
    inside = lax.broadcasted_iota(jnp.int32, (T, W), 1) < limit
    y_ref[:T, :] = jnp.where(inside, y_ref[:T, :], F32(0))
    ohi[...], olo[...] = split(y_ref[...])


def solve_rows(meta, inverse, x):
    whole = pl.BlockSpec((W, W), lambda i, m: (0, 0))
    out = pl.BlockSpec((B, W), lambda i, m: (i, 0))
    return pl.pallas_call(
        solve_rows_kernel,
        grid_spec=pltpu.PrefetchScalarGridSpec(
            num_scalar_prefetch=1,
            grid=(4,),
            in_specs=[
                whole,
                whole,
                pl.BlockSpec((8, 2, T, T), lambda i, m: (0, i, 0, 0)),
            ],
            out_specs=[out, out, pl.BlockSpec((2, T, T), lambda i, m: (i, 0, 0))],
            scratch_shapes=[pltpu.VMEM((B, W), F32)],
        ),
        out_shape=[jax.ShapeDtypeStruct((W, W), BF16)] * 2 + [jax.ShapeDtypeStruct((8, T, T), F32)],
        compiler_params=params(),
        name="solve_rows",
    )(meta, *inverse, x)


def finish_kernel(meta, front, lhi, llo, chi, clo, pan, *rest):
    tiles, (out, p_ref) = rest[:-2], rest[-2:]
    for n in range(0, 2048, 512):
        cols = slice(n, n + 512)
        p_ref[:, cols] = dot3((lhi[...], llo[...]), (chi[:, cols], clo[:, cols]))
    flat_in = front.reshape(2 * T * 16, T)
    flat = out.reshape(2 * T * 16, T)
    for a in range(2):
        for lc in range(16):
            at = ((lc % 2) * 8 + lc // 2) * T
            where = pl.ds(a * T * 16 + lc, T, stride=16)
            flat[where, :] = flat_in[where, :] - p_ref[a * T : (a + 1) * T, at : at + T]
        row_tile = 2 * pl.program_id(0) + a
        for h in range(2):
            _, found = level_of(meta, h, row_tile)

            @pl.when(found == 1)
            def _():
                for kb in range(4):
                    got = tiles[(a * 2 + h) * 4 + kb]
                    for i in range(2):
                        where = pl.ds(a * T * 16 + local_col(meta, h, kb, i), T, stride=16)
                        flat[where, :] = flat[where, :] + got[i]

        kept = (row_tile == 0) & (meta[ROW_AT] < 4) & (meta[COL_AT] >= 4)

        @pl.when(jnp.logical_not(kept))
        def _():
            flat[pl.ds(a * T * 16, T, stride=16), :] = pan[a]


def finish(meta, front, rows, cols, pan, landed):
    def tile_spec(a, h, kb):
        return pl.BlockSpec(
            (None, None, None, 2, T, T),
            lambda i, m: (source_col(m, h, kb), h, level_of(m, h, 2 * i + a)[0], 0, 0, 0),
        )

    whole = pl.BlockSpec((W, 2048), lambda i, m: (0, 0))
    lhs = pl.BlockSpec((B, W), lambda i, m: (i, 0))
    block = pl.BlockSpec((2, T, 16, T), lambda i, m: (i, 0, 0, 0))
    specs = [tile_spec(a, h, kb) for a in range(2) for h in range(2) for kb in range(4)]
    return pl.pallas_call(
        finish_kernel,
        grid_spec=pltpu.PrefetchScalarGridSpec(
            num_scalar_prefetch=1,
            grid=(4,),
            in_specs=[block, lhs, lhs, whole, whole, pl.BlockSpec((2, T, T), lambda i, m: (i, 0, 0))]
            + specs,
            out_specs=block,
            scratch_shapes=[pltpu.VMEM((B, 2048), F32)],
        ),
        out_shape=jax.ShapeDtypeStruct(front.shape, F32),
        compiler_params=params(),
        name="finish",
    )(meta, front, *rows, *cols, pan, *([landed] * 16))


def spread(x, axis, n):
    copies = jnp.broadcast_to(x[None], (n,) + x.shape)
    return lax.all_to_all(copies, axis, split_axis=0, concat_axis=0, tiled=True)


def exchange(x, axis):
    return lax.all_to_all(x, axis, split_axis=0, concat_axis=0, tiled=True)


def shards(front, child_blocks, child_map):
    row = lax.axis_index("row")
    col = lax.axis_index("col")
    meta = jnp.concatenate([child_map.reshape(-1), jnp.stack([row, col])]).astype(jnp.int32)
    lower_half = row < 8

    arrived = exchange(pack_rows(meta, child_blocks), "row")
    got = exchange(pack_cols(meta, arrived, 1), "col")
    first = first_row(meta, front, got)

    down = [(i, i + 8) for i in range(8)]
    ours = jnp.where(lower_half, first[:8], lax.ppermute(first[8:], "row", down))
    pivot = jnp.where(lower_half, first[0, :64], lax.ppermute(first[0, 64:], "row", down))

    pivots = spread(spread(pivot, "col", 8), "row", 16)
    inverse = invert(pivots)

    cols_x = lax.all_gather(ours, "row").reshape(2, 8, 8, T, T)
    turn = [
        ((q + 8 * t) * 8 + c, (c + 8 * t) * 8 + q)
        for t in range(2)
        for q in range(8)
        for c in range(8)
    ]
    turned = lax.ppermute(jnp.swapaxes(ours, 1, 2), ("row", "col"), turn)
    rows_x = lax.all_gather(turned, "col")

    landed = exchange(pack_cols(meta, arrived, 4), "col")

    cols_l = solve_cols(inverse, cols_x)
    *rows_l, pan = solve_rows(meta, inverse, rows_x)
    return finish(meta, front, rows_l, cols_l, pan, landed)


def solution(mesh):
    in_specs = (P(None, "row", None, "col"), P(None, None, "row", None, "col"), P())
    out_specs = P(None, "row", None, "col")
    return jax.shard_map(shards, mesh=mesh, in_specs=in_specs, out_specs=out_specs, check_vma=False)
```

time: 1350 us -> 634 us (0.47)
  waiting for transfers between devices: 769 us -> 42.9 us
  Pallas kernels: 0 us -> 394 us
  other arithmetic: 304 us -> 2.46 us
  blocking collectives: 0 us -> 147 us
  matrix products: 121 us -> 0 us
  local copies, waits for them, and re-layouts: 110 us -> 6.17 us
    psum x4 -> x0, waiting for transfers between devices: 537 us -> none  [the longest x2 282 us: shards(): lax.psum(jnp.stack(diag_pieces, axis=1), 'col')]
    pallas_call x0 -> x8, Pallas kernels: none -> 394 us  [the longest x1 165 us: invert(): pl.pallas_call(invert_kernel, out_shape=[jax.ShapeDtypeStruct((W, W), BF1...]
    another operation x41 -> x0, other arithmetic: 251 us -> none  [the longest x30 159 us: shards(): lower = jnp.linalg.cholesky(diagonal)]
    all_to_all x2, waiting for transfers between devices: 232 us -> 0.01 us  [the longest x1 0.01 us: spread(): return lax.all_to_all(copies, axis, split_axis=0, concat_axis=0, tiled=True)]
    all_to_all x0 -> x3, blocking collectives: none -> 147 us  [the longest x2 135 us: exchange(): return lax.all_to_all(x, axis, split_axis=0, concat_axis=0, tiled=True)]
    dot_general x7 -> x0, matrix products: 80.2 us -> none  [the longest x5 49.8 us: mixed(): jnp.einsum(form, left, right, precision=HIGHEST_PRECISION, preferred_elem...]
    ppermute x0 -> x3, waiting for transfers between devices: none -> 42.2 us  [the longest x1 32.5 us: shards(): turned = lax.ppermute(jnp.swapaxes(ours, 1, 2), ('row', 'col'), turn)]
    unnamed x43 -> x2, local copies, waits for them, and re-layouts: 41.6 us -> 0.01 us
  transfers between devices with their start and end apart: 6 -> 7, of which waited for: 6 -> 3; matrix products, arithmetic and copies ran while one was open for 2% -> 1% of each run, Pallas kernels for 0% -> 50%
where the time goes in v1:
time: 634 us; the launch traced here: 632 us
  Pallas kernels  394 us (62%)
  blocking collectives  147 us (23%)
  waiting for transfers between devices  42.9 us (7%)
  starting transfers between devices  25.8 us (4%)
  between operations  13.5 us (2%)
    pallas_call x1, Pallas kernels, invert(): pl.pallas_call(invert_kernel, out_shape=[jax.ShapeDtypeStruct((W, W), BF1...  165 us
    pallas_call x2, Pallas kernels, pack_cols(): pl.pallas_call(functools.partial(pack_cols_kernel, levels), in_specs=[pl....  163 us
    all_to_all x2, blocking collectives, exchange(): return lax.all_to_all(x, axis, split_axis=0, concat_axis=0, tiled=True)  135 us
    ppermute x1, waiting for transfers between devices, shards(): turned = lax.ppermute(jnp.swapaxes(ours, 1, 2), ('row', 'col'), turn)  32.5 us
    pallas_call x1, Pallas kernels, finish(): pl.pallas_call(finish_kernel, grid_spec=pltpu.PrefetchScalarGridSpec(num_...  30.1 us
    pallas_call x1, Pallas kernels, solve_cols(): pl.pallas_call(solve_cols_kernel, grid=(8,), in_specs=[whole, whole, pl.B...  14.8 us
  transfers between devices with their start and end apart: 7, of which 3 were waited for; matrix products, arithmetic and copies ran while one was open for 1% of the time, Pallas kernels for 50%

profile of v1, /device:TPU:1, one launch (start us, length us, event | category | flops | bytes accessed | tf_op | source)
XLA Modules:
  0.0 632.3 jit_solution(14730475463623475079)
XLA Ops:
  6.5 0.8 reshape.8
  7.3 0.6 pad_add_fusion.meta
  7.9 7.5 %pack_rows.1 = f32[16,8,128,128]{3,2,1,0:T(8,128)} custom-call(s32[130]{0:T(256)} %pad_add_fusion.meta, f32[2,4,128,8,128]{4,3,2,1,0:T(8,128)} %child_ref.1), custom_call_target="tpu_custom_call" | custom-call | tf_op jit(solution)/shard_map/pack_rows/pallas_call | solution.py:81
  15.4 102.0 %all_to_all.25.arrived = f32[16,8,128,128]{3,2,1,0:T(8,128)} all-to-all(f32[16,8,128,128]{3,2,1,0:T(8,128)} %pack_rows.1), channel_id=1, replica_groups=mesh['row'=16,'col'=8] {'row'}, dimensions={0} | all-to-all | bytes 16777216 | tf_op jit(solution)/shard_map/all_to_all | solution.py:376
  117.4 33.6 %pack_cols_1.1 = f32[8,2,1,2,128,128]{5,4,3,2,1,0:T(8,128)} custom-call(s32[130]{0:T(256)} %pad_add_fusion.meta, f32[16,8,128,128]{3,2,1,0:T(8,128)} %all_to_all.25.arrived), custom_call_target="tpu_custom_call" | custom-call | tf_op jit(solution)/shard_map/pack_cols_1/pallas_call | solution.py:121
  151.1 32.8 %all_to_all.26.got_ref = f32[8,2,1,2,128,128]{5,4,3,2,1,0:T(8,128)} all-to-all(f32[8,2,1,2,128,128]{5,4,3,2,1,0:T(8,128)} %pack_cols_1.1), channel_id=1, replica_groups=mesh['row'=16,'col'=8] {'col'}, dimensions={0} | all-to-all | bytes 4194304 | tf_op jit(solution)/shard_map/all_to_all | solution.py:376
  183.9 4.1 first_row.1
  188.0 1.1 slice.19
  189.0 2.2 collective-permute-start.1
  191.3 8.7 %collective-permute-done.1 = f32[8,128,128]{2,1,0:T(8,128)S(1)} collective-permute-done((f32[8,128,128]{2,1,0:T(8,128)S(1)}, f32[8,128,128]{2,1,0:T(8,128)S(1)}, u32[]{:S(2)}, u32[]{:S(2)}) %collective-permute-start.1) | collective-permute-done | bytes 524320 | tf_op jit(solution)/shard_map/ppermute | solution.py:390
  199.9 1.1 slice_select_fusion
  201.0 7.6 %collective-permute-start.2 = (f32[8,128,128]{1,2,0:T(8,128)S(1)}, f32[8,128,128]{1,2,0:T(8,128)S(1)}, u32[]{:S(2)}, u32[]{:S(2)}) collective-permute-start(f32[8,128,128]{1,2,0:T(8,128)S(1)} %bitcast.13), channel_id=1, source_target_pairs={{0,0},{1,8},{2,16},{3,24},{4,32},{5,40},{6,48},{7,56},{8,1},{9,9},... | collective-permute-start | bytes 1572872 | tf_op jit(solution)/shard_map/ppermute | solution.py:403
  208.7 32.5 %collective-permute-done.2 = f32[8,128,128]{1,2,0:T(8,128)S(1)} collective-permute-done((f32[8,128,128]{1,2,0:T(8,128)S(1)}, f32[8,128,128]{1,2,0:T(8,128)S(1)}, u32[]{:S(2)}, u32[]{:S(2)}) %collective-permute-start.2) | collective-permute-done | bytes 524320 | tf_op jit(solution)/shard_map/ppermute | solution.py:403
  241.2 1.0 copy.5
  242.2 0.0 all-gather.5.cloned.1.call-update
  242.2 0.0 all-gather.7.cloned.1.call-start
  242.3 0.7 all-gather.7.cloned.1.call-update
  243.0 0.8 slice_bitcast_fusion
  243.7 5.6 collective-permute-start
  249.4 1.0 collective-permute-done
  250.4 0.8 fusion
  251.2 12.2 %all_to_all.27 = f32[8,64,128]{2,1,0:T(8,128)S(1)} all-to-all(f32[8,64,128]{2,1,0:T(8,128)S(1)} %broadcast_in_dim.4), channel_id=1, replica_groups=mesh['row'=16,'col'=8] {'col'}, dimensions={0} | all-to-all | bytes 524288 | tf_op jit(solution)/shard_map/all_to_all | solution.py:372
  263.4 2.5 broadcast_in_dim.5
  265.9 5.2 all-to-all-start.3
  271.1 129.1 %pack_cols_4.1 = f32[8,2,4,2,128,128]{5,4,3,2,1,0:T(8,128)} custom-call(s32[130]{0:T(256)} %pad_add_fusion.meta, f32[16,8,128,128]{3,2,1,0:T(8,128)} %all_to_all.25.arrived), custom_call_target="tpu_custom_call" | custom-call | tf_op jit(solution)/shard_map/pack_cols_4/pallas_call | solution.py:121
  400.3 0.0 all-to-all-done.3.pieces
  400.3 5.0 all-to-all-start.4
  405.3 165.0 %invert.1 = (bf16[1024,1024]{1,0:T(8,128)(2,1)}, bf16[1024,1024]{1,0:T(8,128)(2,1)}) custom-call(f32[16,8,64,128]{3,2,1,0:T(8,128)} %all-to-all-done.3.pieces), custom_call_target="tpu_custom_call" | custom-call | flops 80000000000 | bytes 8388608 | tf_op jit(solution)/shard_map/invert/pallas_call | solution.py:223
  570.3 10.2 %solve_rows.1 = (bf16[1024,1024]{1,0:T(8,128)(2,1)}, bf16[1024,1024]{1,0:T(8,128)(2,1)}, f32[8,128,128]{2,1,0:T(8,128)}) custom-call(s32[130]{0:T(256)} %pad_add_fusion.meta, bf16[1024,1024]{1,0:T(8,128)(2,1)} %get-tuple-element.12.ihi, bf16[1024,1024]{1,0:T(8,128)(2,1)} %get-tuple-element.13.ilo, f32[8,8,128,128]{3,2,1,0:T(8,128)} %bitcast.12), custom_call_target="tpu_custom_call" | custom-call | tf_op jit(solution)/shard_map/solve_rows/pallas_call | solution.py:293
  580.5 14.8 %solve_cols.1 = (bf16[1024,2048]{1,0:T(8,128)(2,1)}, bf16[1024,2048]{1,0:T(8,128)(2,1)}) custom-call(bf16[1024,1024]{1,0:T(8,128)(2,1)} %get-tuple-element.12.ihi, bf16[1024,1024]{1,0:T(8,128)(2,1)} %get-tuple-element.13.ilo, f32[2,8,8,128,128]{4,3,2,1,0:T(8,128)} %bitcast.11), custom_call_target="tpu_custom_call" | custom-call | tf_op jit(solution)/shard_map/solve_cols/pallas_call | solution.py:255
  595.3 0.0 all-to-all-done.4.rest_0_.rest_1_.rest_2_.rest_3_.rest_4_.rest_5_.rest_6_.rest_7_.rest_8_.rest_9_.rest_10_.rest_11_.rest_12_.rest_13_.rest_14_.rest_15_
  595.3 30.1 %finish.1 = f32[8,128,16,128]{3,2,1,0:T(8,128)} custom-call(s32[130]{0:T(256)} %pad_add_fusion.meta, f32[8,128,16,128]{3,2,1,0:T(8,128)} %front.1, bf16[1024,1024]{1,0:T(8,128)(2,1)} %get-tuple-element.14.lhi, bf16[1024,1024]{1,0:T(8,128)(2,1)} %get-tuple-element.15.llo, bf16[1024,2048]{1,0:T(8,128)(2,1)} %get-tuple-element.16.chi, ...), custom_call_target="tpu_custom_call" | custom-call | tf_op jit(solution)/shard_map/finish/pallas_call | solution.py:354
  (6 shorter events, 0.0 us)
Async XLA Ops:
  6.5 563.8 %all-gather.5.cloned.1.call-start = ((), (), s32[]{:S(2)}) async-start(), calls=%async_computation.5 | async-start | bytes 4718592 | tf_op jit(solution)/shard_map/all_gather | solution.py:404
  189.0 10.9 %collective-permute-start.1 = (f32[8,128,128]{2,1,0:T(8,128)S(1)}, f32[8,128,128]{2,1,0:T(8,128)S(1)}, u32[]{:S(2)}, u32[]{:S(2)}) collective-permute-start(f32[8,128,128]{2,1,0:T(8,128)S(1)} %slice.19), channel_id=1, source_target_pairs={{0,64},{8,72},{16,80},{24,88},{32,96},{40,104},{48,112},{56,120},{... | collective-permute-start | bytes 1572872 | tf_op jit(solution)/shard_map/ppermute | solution.py:390
  201.0 41.2 %copy-start = (f32[8,128,128]{2,1,0:T(8,128)}, f32[8,128,128]{2,1,0:T(8,128)S(1)}, u32[]{:S(2)}) copy-start(f32[8,128,128]{2,1,0:T(8,128)S(1)} %slice_select_fusion) | copy-start | bytes 1572868
  201.0 40.1 %collective-permute-start.2 = (f32[8,128,128]{1,2,0:T(8,128)S(1)}, f32[8,128,128]{1,2,0:T(8,128)S(1)}, u32[]{:S(2)}, u32[]{:S(2)}) collective-permute-start(f32[8,128,128]{1,2,0:T(8,128)S(1)} %bitcast.13), channel_id=1, source_target_pairs={{0,0},{1,8},{2,16},{3,24},{4,32},{5,40},{6,48},{7,56},{8,1},{9,9},... | collective-permute-start | bytes 1572872 | tf_op jit(solution)/shard_map/ppermute | solution.py:403
  242.2 338.3 %all-gather.7.cloned.1.call-start = ((), (), s32[]{:S(2)}) async-start(), calls=%async_computation.6 | async-start | bytes 8912896 | tf_op jit(solution)/shard_map/all_gather | solution.py:396
  243.7 6.7 %collective-permute-start = (f32[64,128]{1,0:T(8,128)S(1)}, f32[64,128]{1,0:T(8,128)S(1)}, u32[]{:S(2)}, u32[]{:S(2)}) collective-permute-start(f32[64,128]{1,0:T(8,128)S(1)} %slice_bitcast_fusion), channel_id=1, source_target_pairs={{0,64},{8,72},{16,80},{24,88},{32,96},{40,104},{48,112},{56,120},{... | collective-permute-start | bytes 98312 | tf_op jit(solution)/shard_map/ppermute | solution.py:391
  265.9 134.3 %all-to-all-start.3 = ((f32[16,8,64,128]{3,2,1,0:T(8,128)}), f32[16,8,64,128]{3,2,1,0:T(8,128)}, u32[]{:S(2)}, u32[]{:S(2)}) async-start(f32[16,8,64,128]{3,2,1,0:T(8,128)} %broadcast_in_dim.5), calls=%async_computation.3 | async-start | bytes 8388608 | tf_op jit(solution)/shard_map/all_to_all | solution.py:372
  400.3 195.0 %all-to-all-start.4 = ((f32[8,2,4,2,128,128]{5,4,3,2,1,0:T(8,128)}), f32[8,2,4,2,128,128]{5,4,3,2,1,0:T(8,128)}, u32[]{:S(2)}, u32[]{:S(2)}) async-start(f32[8,2,4,2,128,128]{5,4,3,2,1,0:T(8,128)} %pack_cols_4.1), calls=%async_computation.4 | async-start | bytes 16777216 | tf_op jit(solution)/shard_map/all_to_all | solution.py:376
Sparse Core Ops, SparseCore 0:
  242.3 95.2 all-gather.4
  339.4 76.7 all-gather.6

commit v2 on v1

v2 whole, which is shorter than its diff:
```python
import functools

import jax
import jax.numpy as jnp
from jax import lax
from jax.experimental import pallas as pl
from jax.experimental.pallas import tpu as pltpu
from jax.sharding import PartitionSpec as P

T = 128
W = 1024
F32 = jnp.float32
BF16 = jnp.bfloat16
HIGHEST = lax.Precision.HIGHEST
ROW_AT = 128
COL_AT = 129
VMEM = 58 * 1024 * 1024


def params(**kw):
    return pltpu.CompilerParams(vmem_limit_bytes=VMEM, **kw)


def shift(meta, h, k):
    return meta[h * 64 + 16 * k] & 15


def source_row(meta, h, ka):
    return (meta[ROW_AT] - shift(meta, h, ka)) & 15


def local_row(meta, h, ka):
    return meta[h * 64 + source_row(meta, h, ka) + 16 * ka] >> 4


def level_of(meta, h, a):
    ka = jnp.int32(0)
    found = jnp.int32(0)
    for k in range(4):
        hit = local_row(meta, h, k) == a
        ka = jnp.where(hit, k, ka)
        found = jnp.where(hit, 1, found)
    return ka, found


def dest_col(meta, h, kb):
    return (meta[COL_AT] + shift(meta, h, kb)) & 7


def source_col(meta, h, kb):
    return (meta[COL_AT] - shift(meta, h, kb)) & 7


def local_col(meta, h, kb, i):
    return meta[h * 64 + source_col(meta, h, kb) + 8 * (2 * kb + i)] >> 3


def split(x):
    hi = x.astype(BF16)
    return hi, (x - hi.astype(F32)).astype(BF16)


def dot(a, b, dims=((1,), (0,)), precision=None):
    return lax.dot_general(a, b, (dims, ((), ())), precision=precision, preferred_element_type=F32)


NT = ((1,), (1,))


def dot3(a, b, dims=((1,), (0,))):
    return dot(a[0], b[0], dims) + (dot(a[0], b[1], dims) + dot(a[1], b[0], dims))


def pack_rows_kernel(meta, child_ref, out_ref):
    flat = child_ref.reshape(T * 8, T)
    for j in range(8):
        out_ref[0, j] = flat[pl.ds(j, T, stride=8), :]


def pack_rows(meta, child):
    return pl.pallas_call(
        pack_rows_kernel,
        grid_spec=pltpu.PrefetchScalarGridSpec(
            num_scalar_prefetch=1,
            grid=(2, 4),
            in_specs=[pl.BlockSpec((None, None, T, 8, T), lambda h, k, m: (h, k, 0, 0, 0))],
            out_specs=pl.BlockSpec(
                (1, 8, T, T), lambda h, k, m: ((m[ROW_AT] + shift(m, h, k)) & 15, 0, 0, 0)
            ),
        ),
        out_shape=jax.ShapeDtypeStruct((16, 8, T, T), F32),
        compiler_params=params(),
        name="pack_rows",
    )(meta, child)


def pack_cols_kernel(meta, *refs):
    for lev in range(4):
        refs[4][lev] = refs[lev][...]


def pack_cols(meta, arrived):
    def source(lev):
        return pl.BlockSpec((None, 2, T, T), lambda h, kb, m: (source_row(m, h, lev), kb, 0, 0))

    return pl.pallas_call(
        pack_cols_kernel,
        grid_spec=pltpu.PrefetchScalarGridSpec(
            num_scalar_prefetch=1,
            grid=(2, 4),
            in_specs=[source(lev) for lev in range(4)],
            out_specs=pl.BlockSpec(
                (None, None, 4, 2, T, T), lambda h, kb, m: (dest_col(m, h, kb), h, 0, 0, 0, 0)
            ),
        ),
        out_shape=jax.ShapeDtypeStruct((8, 2, 4, 2, T, T), F32),
        compiler_params=params(),
        name="pack_cols",
    )(meta, *([arrived] * 4))


def place(lc):
    return (lc & 1) * 8 + (lc >> 1)


def assemble_kernel(start, meta, front_ref, *refs):
    tiles, out_ref = refs[:-1], refs[-1]
    flat = front_ref.reshape(T * 16, T)
    for lc in range(16):
        out_ref[place(lc)] = flat[pl.ds(lc, T, stride=16), :]
    for h in range(2):
        _, found = level_of(meta, h, start + pl.program_id(0))

        @pl.when(found == 1)
        def _():
            for kb in range(4):
                for i in range(2):
                    at = place(local_col(meta, h, kb, i))
                    out_ref[at] = out_ref[at] + tiles[4 * h + kb][i]


def assemble(meta, front, landed, start, count):
    def tile_spec(h, kb):
        return pl.BlockSpec(
            (None, None, None, 2, T, T),
            lambda i, m: (source_col(m, h, kb), h, level_of(m, h, start + i)[0], 0, 0, 0),
        )

    return pl.pallas_call(
        functools.partial(assemble_kernel, start),
        grid_spec=pltpu.PrefetchScalarGridSpec(
            num_scalar_prefetch=1,
            grid=(count,),
            in_specs=[pl.BlockSpec((None, T, 16, T), lambda i, m: (start + i, 0, 0, 0))]
            + [tile_spec(h, kb) for h in range(2) for kb in range(4)],
            out_specs=pl.BlockSpec((None, 16, T, T), lambda i, m: (i, 0, 0, 0)),
        ),
        out_shape=jax.ShapeDtypeStruct((count, 16, T, T), F32),
        compiler_params=params(),
        cost_estimate=pl.CostEstimate(flops=0, bytes_accessed=count * 5 << 19, transcendentals=0),
        name=f"assemble_{count}",
    )(meta, front, *([landed] * 8))


def root(x):
    r = lax.rsqrt(x)
    return r * (1.5 - 0.5 * x * r * r)


def inverse_of(x):
    r = pl.reciprocal(x, approx=True)
    r = r * (2.0 - x * r)
    return r * (2.0 - x * r)


def invert_kernel(meta, own, other, hi_ref, lo_ref, a_ref, t_ref, l_ref):
    row, col = meta[ROW_AT], meta[COL_AT]
    for q in range(8):
        same = ((row ^ q) & 1) == 0
        dz = ((row >> 1) - (q >> 1)) & 3
        for c in range(8):
            at = (dz, ((col >> 1) - (c >> 1)) & 3, (col ^ c) & 1)
            a_ref[q * T : (q + 1) * T, c * T : (c + 1) * T] = jnp.where(same, own[at], other[at])
    t_ref[...] = jnp.zeros_like(t_ref)
    sub = lax.broadcasted_iota(jnp.int32, (8, T), 0)
    lane = lax.broadcasted_iota(jnp.int32, (8, T), 1)

    def over(x):
        return jnp.broadcast_to(x, (8, T))

    def step(k, _):
        at = pl.multiple_of(k * T, T)
        s = [a_ref[pl.ds(at + 8 * b, 8), pl.ds(at, T)] for b in range(16)]
        on_diagonal = [lane == sub + 8 * b for b in range(16)]
        only = [jnp.where(on_diagonal[b], s[b], F32(0)) for b in range(16)]
        total = only[0]
        for b in range(1, 16):
            total = total + only[b]
        by_lane = over(root(jnp.sum(total, axis=0, keepdims=True)))
        s = [s[b] * (over(root(jnp.sum(only[b], axis=1, keepdims=True))) * by_lane) for b in range(16)]
        t = [jnp.where(on_diagonal[b], F32(1), F32(0)) for b in range(16)]
        for j in range(0, T, 4):
            b0, i0 = divmod(j, 8)
            p = [[over(s[b0][i0 + i : i0 + i + 1, j + c : j + c + 1]) for c in range(i + 1)] for i in range(4)]
            sr = [over(s[b0][i0 + i : i0 + i + 1, :]) for i in range(4)]
            tr = [over(t[b0][i0 + i : i0 + i + 1, :]) for i in range(4)]
            (p00,), (p10, p11), (p20, p21, p22), (p30, p31, p32, p33) = p
            first = inverse_of(p00 * p11 - p10 * p10)
            x20 = (p20 * p11 - p21 * p10) * first
            x21 = (p21 * p00 - p20 * p10) * first
            x30 = (p30 * p11 - p31 * p10) * first
            x31 = (p31 * p00 - p30 * p10) * first
            s22 = p22 - (x20 * p20 + x21 * p21)
            s32 = p32 - (x30 * p20 + x31 * p21)
            s33 = p33 - (x30 * p30 + x31 * p31)
            second = inverse_of(s22 * s33 - s32 * s32)
            y00, y10, y11 = p11 * first, p10 * first, p00 * first
            y22, y32, y33 = s33 * second, s32 * second, s22 * second

            def solved(rows):
                r2 = rows[2] - (x20 * rows[0] + x21 * rows[1])
                r3 = rows[3] - (x30 * rows[0] + x31 * rows[1])
                z2 = y22 * r2 - y32 * r3
                z3 = y33 * r3 - y32 * r2
                z0 = (y00 * rows[0] - y10 * rows[1]) - (x20 * z2 + x30 * z3)
                z1 = (y11 * rows[1] - y10 * rows[0]) - (x21 * z2 + x31 * z3)
                return (z0, z1, z2, z3), r2, r3

            zs, _, _ = solved(sr)
            zt, t2, t3 = solved(tr)
            r0 = root(p00)
            l10 = p10 * r0
            r1 = root(p11 - l10 * l10)
            r2 = root(s22)
            l32 = s32 * r2
            r3 = root(s33 - l32 * l32)
            done = (
                tr[0] * r0,
                (tr[1] - l10 * r0 * tr[0]) * r1,
                t2 * r2,
                (t3 - l32 * r2 * t2) * r3,
            )
            for b in range(b0 if i0 == 0 else b0 + 1, 16):
                v = [over(s[b][:, j + c : j + c + 1]) for c in range(4)]
                if b == b0:
                    v = [jnp.where(sub > 3, x, F32(0)) for x in v]
                s[b] = s[b] - ((v[0] * zs[0] + v[1] * zs[1]) + (v[2] * zs[2] + v[3] * zs[3]))
                t[b] = t[b] - ((v[0] * zt[0] + v[1] * zt[1]) + (v[2] * zt[2] + v[3] * zt[3]))
            for i in range(4):
                t[b0] = jnp.where(sub == i0 + i, done[i], t[b0])
        t = [x * by_lane for x in t]
        kinv = jnp.concatenate(t, axis=0)
        for kk in range(8):

            @pl.when(k == kk)
            def _():
                lo, hi = kk * T, (kk + 1) * T
                if kk:
                    t_ref[lo:hi, :lo] = dot(kinv, t_ref[lo:hi, :lo], precision=HIGHEST)
                t_ref[lo:hi, lo:hi] = kinv
                if kk < 7:
                    col = dot(a_ref[hi:, lo:hi], kinv, NT, precision=HIGHEST)
                    l_ref[hi:, :] = col
                    for n0 in range(hi, W, T):
                        a_ref[n0:, n0 : n0 + T] = a_ref[n0:, n0 : n0 + T] - dot(
                            l_ref[n0:, :], l_ref[n0 : n0 + T, :], NT, precision=HIGHEST
                        )
                    t_ref[hi:, :hi] = t_ref[hi:, :hi] - dot(
                        l_ref[hi:, :], t_ref[lo:hi, :hi], precision=HIGHEST
                    )

        return 0

    lax.fori_loop(0, 8, step, 0)
    hi_ref[...], lo_ref[...] = split(t_ref[...])


def invert(meta, own, other):
    whole = pl.BlockSpec(memory_space=pltpu.VMEM)
    return pl.pallas_call(
        invert_kernel,
        in_specs=[pl.BlockSpec(memory_space=pltpu.SMEM), whole, whole],
        out_specs=[whole, whole],
        out_shape=[jax.ShapeDtypeStruct((W, W), BF16)] * 2,
        scratch_shapes=[
            pltpu.VMEM((W, W), F32),
            pltpu.VMEM((W, W), F32),
            pltpu.VMEM((W, T), F32),
        ],
        compiler_params=params(),
        cost_estimate=pl.CostEstimate(flops=80_000_000_000, bytes_accessed=8 << 20, transcendentals=0),
        name="invert",
    )(meta, own, other)


B = 256


def solve_cols_kernel(ihi, ilo, x_ref, ohi, olo, y_ref):
    for k in range(W // B):
        x = jnp.concatenate(
            [jnp.concatenate([x_ref[q, 0], x_ref[q, 1]], axis=1) for q in (2 * k, 2 * k + 1)], axis=0
        )
        cols = slice(k * B, (k + 1) * B)
        y = dot3((ihi[k * B :, cols], ilo[k * B :, cols]), split(x))
        y_ref[k * B :, :] = y if k == 0 else y_ref[k * B :, :] + y
        ohi[cols, :], olo[cols, :] = split(y_ref[cols, :])


def solve_cols(inverse, x):
    whole = pl.BlockSpec((W, W), lambda i: (0, 0))
    out = pl.BlockSpec((W, B), lambda i: (0, i))
    return pl.pallas_call(
        solve_cols_kernel,
        grid=(8,),
        in_specs=[
            whole,
            whole,
            pl.BlockSpec((None, 8, 2, T, T), lambda i: (i // 4, 0, i % 4, 0, 0)),
        ],
        out_specs=[out, out],
        out_shape=[jax.ShapeDtypeStruct((W, 2048), BF16)] * 2,
        scratch_shapes=[pltpu.VMEM((W, B), F32)],
        compiler_params=params(),
        name="solve_cols",
    )(*inverse, x)


H = 4


def solve_rows_kernel(meta, ihi, ilo, *refs):
    xs, (ohi, olo, pan, xhi, xlo, y_ref) = refs[:4], refs[4:]
    for d in range(8):
        q = (((meta[COL_AT] >> 1) - (d >> 1)) & 3) * 2 + ((meta[COL_AT] ^ d) & 1)
        cols = pl.ds(pl.multiple_of(q * T, T), T)
        for a in range(H):
            rows = slice(a * T, (a + 1) * T)
            xhi[rows, cols], xlo[rows, cols] = split(xs[d >> 1][d & 1, a])
    for k in range(W // B):
        n = (k + 1) * B
        rows = slice(k * B, n)
        y_ref[:, rows] = dot3((xhi[:, :n], xlo[:, :n]), (ihi[rows, :n], ilo[rows, :n]), NT)
    at = pl.multiple_of(meta[COL_AT] * T, T)
    for a in range(H):
        pan[a] = y_ref[a * T : (a + 1) * T, pl.ds(at, T)]
    row = meta[ROW_AT]
    limit = jnp.where(row < 4, 0, jnp.where(row < 8, 512, W))
    limit = jnp.where(pl.program_id(0) == 0, limit, W)
    inside = lax.broadcasted_iota(jnp.int32, (T, W), 1) < limit
    y_ref[:T, :] = jnp.where(inside, y_ref[:T, :], F32(0))
    ohi[...], olo[...] = split(y_ref[...])


def solve_rows(meta, inverse, xs):
    whole = pl.BlockSpec((W, W), lambda i, m: (0, 0))
    out = pl.BlockSpec((H * T, W), lambda i, m: (i, 0))
    tiles = pl.BlockSpec((H, T, T), lambda i, m: (i, 0, 0))
    return pl.pallas_call(
        solve_rows_kernel,
        grid_spec=pltpu.PrefetchScalarGridSpec(
            num_scalar_prefetch=1,
            grid=(8 // H,),
            in_specs=[whole, whole] + [pl.BlockSpec((2, H, T, T), lambda i, m: (0, i, 0, 0))] * 4,
            out_specs=[out, out, tiles],
            scratch_shapes=[
                pltpu.VMEM((H * T, W), BF16),
                pltpu.VMEM((H * T, W), BF16),
                pltpu.VMEM((H * T, W), F32),
            ],
        ),
        out_shape=[jax.ShapeDtypeStruct((W, W), BF16)] * 2 + [jax.ShapeDtypeStruct((8, T, T), F32)],
        compiler_params=params(),
        name="solve_rows",
    )(meta, *inverse, *xs)


F = 2


def finish_kernel(meta, m_ref, lhi, llo, chi, clo, pan, out):
    flat = out.reshape(F * T * 16, T)
    for n in range(0, 2048, 512):
        cols = slice(n, n + 512)
        p = dot3((lhi[...], llo[...]), (chi[:, cols], clo[:, cols]))
        for a in range(F):
            for at in range(n // T, n // T + 4):
                lc = (at % 8) * 2 + at // 8
                flat[pl.ds(a * T * 16 + lc, T, stride=16), :] = (
                    m_ref[a, at] - p[a * T : (a + 1) * T, (at * T) % 512 : (at * T) % 512 + T]
                )
    for a in range(F):
        kept = (pl.program_id(0) * F + a == 0) & (meta[ROW_AT] < 4) & (meta[COL_AT] >= 4)

        @pl.when(jnp.logical_not(kept))
        def _():
            flat[pl.ds(a * T * 16, T, stride=16), :] = pan[a]


def finish(meta, m, rows, cols, pan):
    whole = pl.BlockSpec((W, 2048), lambda i, m: (0, 0))
    lhs = pl.BlockSpec((F * T, W), lambda i, m: (i, 0))
    return pl.pallas_call(
        finish_kernel,
        grid_spec=pltpu.PrefetchScalarGridSpec(
            num_scalar_prefetch=1,
            grid=(8 // F,),
            in_specs=[
                pl.BlockSpec((F, 16, T, T), lambda i, m: (i, 0, 0, 0)),
                lhs,
                lhs,
                whole,
                whole,
                pl.BlockSpec((F, T, T), lambda i, m: (i, 0, 0)),
            ],
            out_specs=pl.BlockSpec((F, T, 16, T), lambda i, m: (i, 0, 0, 0)),
        ),
        out_shape=jax.ShapeDtypeStruct((8, T, 16, T), F32),
        compiler_params=params(),
        name="finish",
    )(meta, m, *rows, *cols, pan)


def exchange(x, axis):
    return lax.all_to_all(x, axis, split_axis=0, concat_axis=0, tiled=True)


def row_id(y, z, core):
    return (y % 2) * 8 + (z % 4) * 2 + core % 2


def col_id(x, y):
    return (x % 4) * 2 + y % 2


def along_row(v, dy, dz, dcore):
    pairs = [
        (row_id(y, z, core), row_id(y + dy, z + dz, core + dcore))
        for y in range(2)
        for z in range(4)
        for core in range(2)
    ]
    return lax.ppermute(v, "row", pairs)


def along_col(v, dx, dy):
    return lax.ppermute(
        v, "col", [(col_id(x, y), col_id(x + dx, y + dy)) for x in range(4) for y in range(2)]
    )


def down(v):
    return lax.ppermute(v, "row", [(i, i + 8) for i in range(8)])


def shards(front, child_blocks, child_map):
    row = lax.axis_index("row")
    col = lax.axis_index("col")
    meta = jnp.concatenate([child_map.reshape(-1), jnp.stack([row, col])]).astype(jnp.int32)
    upper = row < 8

    arrived = exchange(pack_rows(meta, child_blocks), "row")
    landed = exchange(pack_cols(meta, arrived), "col")
    first = assemble(meta, front, landed, 0, 1)[0]

    tile = jnp.where(upper, first[0], down(first[0]))
    two = jnp.stack([tile, along_col(tile, 0, 1)])
    two, first = lax.optimization_barrier((two, first))
    line = jnp.stack([two] + [along_col(two, dx, 0) for dx in (1, 2, 3)])
    ours = jnp.where(upper, first[:8], down(first[8:]))
    line, landed, front = lax.optimization_barrier((line, landed, front))
    parts = [line] + [along_row(line, 0, dz, 0) for dz in (1, 2, 3)]
    matrix = assemble(meta, front, landed, 0, 8)
    parts, matrix, ours = lax.optimization_barrier((parts, matrix, ours))
    own = jnp.stack(parts)
    other = along_row(own, 0, 0, 1)

    mine = matrix[:, 0]
    pair = jnp.stack([mine, along_col(mine, 0, 1)])
    cols_x = lax.all_gather(ours, "row").reshape(2, 8, 8, T, T)
    other, pair = lax.optimization_barrier((other, pair))
    rows_x = [pair] + [along_col(pair, dx, 0) for dx in (1, 2, 3)]

    inverse = invert(meta, own, other)
    *rows_l, pan = solve_rows(meta, inverse, rows_x)
    cols_l = solve_cols(inverse, cols_x)
    return finish(meta, matrix, rows_l, cols_l, pan)


def solution(mesh):
    in_specs = (P(None, "row", None, "col"), P(None, None, "row", None, "col"), P())
    out_specs = P(None, "row", None, "col")
    return jax.shard_map(shards, mesh=mesh, in_specs=in_specs, out_specs=out_specs, check_vma=False)
```

time: 634 us -> 445 us (0.70)
  Pallas kernels: 394 us -> 156 us
  blocking collectives: 147 us -> 202 us
  starting transfers between devices: 25.8 us -> 19.1 us
    pallas_call x4, Pallas kernels: 332 us -> 101 us  [the longest x1 78 us: invert(): pl.pallas_call(invert_kernel, in_specs=[pl.BlockSpec(memory_space=pltpu.S...]
    all_to_all x2, blocking collectives: 135 us -> 202 us  [exchange(): return lax.all_to_all(x, axis, split_axis=0, concat_axis=0, tiled=True)]
    all_to_all x1 -> x0, blocking collectives: 12.2 us -> none  [spread(): return lax.all_to_all(copies, axis, split_axis=0, concat_axis=0, tiled=True)]
    all_to_all x2 -> x0, starting transfers between devices: 10.2 us -> none  [the longest x1 5.2 us: spread(): return lax.all_to_all(copies, axis, split_axis=0, concat_axis=0, tiled=True)]
    pallas_call x1, Pallas kernels: 30.1 us -> 22.2 us  [finish(): pl.pallas_call(finish_kernel, grid_spec=pltpu.PrefetchScalarGridSpec(num_...]
    ppermute x3 -> x14, starting transfers between devices: 15.5 us -> 19.1 us  [the longest x8 8.32 us: along_col(): lax.ppermute(v, 'col', [(col_id(x, y), col_id(x + dx, y + dy)) for x in r...]
    ppermute x3 -> x14, waiting for transfers between devices: 42.2 us -> 39.8 us  [the longest x8 27.2 us: along_col(): lax.ppermute(v, 'col', [(col_id(x, y), col_id(x + dx, y + dy)) for x in r...]
  transfers between devices with their start and end apart: 7 -> 15, of which waited for: 3 -> 7; matrix products, arithmetic and copies ran while one was open for 1% -> 1% of each run, Pallas kernels for 50% -> 23%
where the time goes in v2:
time: 445 us; the launch traced here: 440 us
  blocking collectives  202 us (45%)
  Pallas kernels  156 us (35%)
  waiting for transfers between devices  39.8 us (9%)
  starting transfers between devices  19.1 us (4%)
  between operations  13.6 us (3%)
  local copies, waits for them, and re-layouts  6.36 us (1%)
    all_to_all x2, blocking collectives, exchange(): return lax.all_to_all(x, axis, split_axis=0, concat_axis=0, tiled=True)  202 us
    pallas_call x1, Pallas kernels, invert(): pl.pallas_call(invert_kernel, in_specs=[pl.BlockSpec(memory_space=pltpu.S...  78 us
    ppermute x8, waiting for transfers between devices, along_col(): lax.ppermute(v, 'col', [(col_id(x, y), col_id(x + dx, y + dy)) for x in r...  27.2 us
    pallas_call x1, Pallas kernels, finish(): pl.pallas_call(finish_kernel, grid_spec=pltpu.PrefetchScalarGridSpec(num_...  22.2 us
    pallas_call x2, Pallas kernels, assemble(): pl.pallas_call(functools.partial(assemble_kernel, start), grid_spec=pltpu...  15.9 us
    pallas_call x1, Pallas kernels, solve_cols(): pl.pallas_call(solve_cols_kernel, grid=(8,), in_specs=[whole, whole, pl.B...  14.8 us
    ppermute x4, waiting for transfers between devices, along_row(): return lax.ppermute(v, 'row', pairs)  11.2 us
    pallas_call x1, Pallas kernels, solve_rows(): pl.pallas_call(solve_rows_kernel, grid_spec=pltpu.PrefetchScalarGridSpec(...  10.6 us
  transfers between devices with their start and end apart: 15, of which 7 were waited for; matrix products, arithmetic and copies ran while one was open for 1% of the time, Pallas kernels for 23%

profile of v2, /device:TPU:1, one launch (start us, length us, event | category | flops | bytes accessed | tf_op | source)
XLA Modules:
  0.0 440.1 jit_solution(1877345856772431801)
XLA Ops:
  7.9 7.5 %pack_rows.1 = f32[16,8,128,128]{3,2,1,0:T(8,128)} custom-call(s32[130]{0:T(256)} %pad_add_fusion.meta, f32[2,4,128,8,128]{4,3,2,1,0:T(8,128)} %child_ref.1), custom_call_target="tpu_custom_call" | custom-call | tf_op jit(solution)/shard_map/pack_rows/pallas_call | solution.py:81
  15.4 102.0 %all_to_all.10.refs_0_.refs_1_.refs_2_.refs_3_ = f32[16,8,128,128]{3,2,1,0:T(8,128)} all-to-all(f32[16,8,128,128]{3,2,1,0:T(8,128)} %pack_rows.1), channel_id=1, replica_groups=mesh['row'=16,'col'=8] {'row'}, dimensions={0} | all-to-all | bytes 16777216 | tf_op jit(solution)/shard_map/all_to_all | solution.py:425
  117.4 7.3 %pack_cols.1 = f32[8,2,4,2,128,128]{5,4,3,2,1,0:T(8,128)} custom-call(s32[130]{0:T(256)} %pad_add_fusion.meta, f32[16,8,128,128]{3,2,1,0:T(8,128)} %all_to_all.10.refs_0_.refs_1_.refs_2_.refs_3_, f32[16,8,128,128]{3,2,1,0:T(8,128)} %all_to_all.10.refs_0_.refs_1_.refs_2_.refs_3_, f32[16,8,128,128]{3,2,1,0:T(8,128)} %all_to_all.10.refs_0_.refs_1_.refs_2_.refs_3_, ...), custom_call_target="tpu_custom_call" | custom-call | tf_op jit(solution)/shard_map/pack_cols/pallas_call | solution.py:106
  124.8 100.2 %all_to_all.11.refs_0_.refs_1_.refs_2_.refs_3_.refs_4_.refs_5_.refs_6_.refs_7_ = f32[8,2,4,2,128,128]{5,4,3,2,1,0:T(8,128)} all-to-all(f32[8,2,4,2,128,128]{5,4,3,2,1,0:T(8,128)} %pack_cols.1), channel_id=1, replica_groups=mesh['row'=16,'col'=8] {'col'}, dimensions={0} | all-to-all | bytes 16777216 | tf_op jit(solution)/shard_map/all_to_all | solution.py:425
  225.0 3.7 assemble_1.1
  228.7 0.8 slice_bitcast_fusion.2
  229.5 3.0 collective-permute-start
  232.6 1.3 collective-permute-done
  233.9 0.8 broadcast_select_fusion
  234.7 2.8 collective-permute-start.1
  237.5 2.4 collective-permute-done.1
  239.9 1.1 slice.16
  241.0 3.2 collective-permute-start.8
  244.2 1.5 collective-permute-start.4
  246.5 0.8 collective-permute-start.2
  247.2 0.9 collective-permute-done.4
  248.1 3.0 collective-permute-done.3
  251.2 1.3 collective-permute-done.2
  252.5 2.0 collective-permute-start.7
  255.2 12.2 %assemble_8.1.m_ref = f32[8,16,128,128]{3,2,1,0:T(8,128)} custom-call(s32[130]{0:T(256)} %pad_add_fusion.meta, f32[8,128,16,128]{3,2,1,0:T(8,128)} %front_ref.2, f32[8,2,4,2,128,128]{5,4,3,2,1,0:T(8,128)} %all_to_all.11.refs_0_.refs_1_.refs_2_.refs_3_.refs_4_.refs_5_.refs_6_.refs_7_, ...), custom_call_target="tpu_custom_call" | custom-call | bytes 20971520 | tf_op jit(solution)/shard_map/assemble_8/pallas_call | solution.py:149
  267.4 0.9 slice_select_fusion
  268.3 11.2 %collective-permute-done.5 = f32[4,2,128,128]{3,2,1,0:T(8,128)S(1)} collective-permute-done((f32[4,2,128,128]{3,2,1,0:T(8,128)S(1)}, f32[4,2,128,128]{3,2,1,0:T(8,128)S(1)}, u32[]{:S(2)}, u32[]{:S(2)}) %collective-permute-start.5) | collective-permute-done | bytes 524320 | tf_op jit(solution)/shard_map/ppermute | solution.py:443
  279.7 1.9 collective-permute-start.9
  281.6 1.1 slice_bitcast_fusion.1
  282.7 2.2 collective-permute-start.10
  285.0 19.6 %collective-permute-done.10 = f32[8,128,128]{2,1,0:T(8,128)S(1)} collective-permute-done((f32[8,128,128]{2,1,0:T(8,128)S(1)}, f32[8,128,128]{2,1,0:T(8,128)S(1)}, u32[]{:S(2)}, u32[]{:S(2)}) %collective-permute-start.10) | collective-permute-done | bytes 524320 | tf_op jit(solution)/shard_map/ppermute | solution.py:447
  304.8 1.3 copy-done.5
  306.2 78.0 %invert.1 = (bf16[1024,1024]{1,0:T(8,128)(2,1)}, bf16[1024,1024]{1,0:T(8,128)(2,1)}) custom-call(s32[130]{0:T(256)} %pad_add_fusion.meta, f32[4,4,2,128,128]{4,3,2,1,0:T(8,128)} %copy-done.2, f32[4,4,2,128,128]{4,3,2,1,0:T(8,128)} %copy-done.5), custom_call_target="tpu_custom_call" | custom-call | flops 80000000000 | bytes 8388608 | tf_op jit(solution)/shard_map/invert/pallas_call | solution.py:280
  384.3 1.0 copy-done.3
  385.6 10.6 %solve_rows.1 = (bf16[1024,1024]{1,0:T(8,128)(2,1)}, bf16[1024,1024]{1,0:T(8,128)(2,1)}, f32[8,128,128]{2,1,0:T(8,128)}) custom-call(s32[130]{0:T(256)} %pad_add_fusion.meta, bf16[1024,1024]{1,0:T(8,128)(2,1)} %get-tuple-element.36.ihi, bf16[1024,1024]{1,0:T(8,128)(2,1)} %get-tuple-element.37.ilo, f32[2,8,128,128]{3,2,1,0:T(8,128)} %copy-done.1, ...), custom_call_target="tpu_custom_call" | custom-call | tf_op jit(solution)/shard_map/solve_rows/pallas_call | solution.py:359
  396.2 14.8 %solve_cols.1 = (bf16[1024,2048]{1,0:T(8,128)(2,1)}, bf16[1024,2048]{1,0:T(8,128)(2,1)}) custom-call(bf16[1024,1024]{1,0:T(8,128)(2,1)} %get-tuple-element.36.ihi, bf16[1024,1024]{1,0:T(8,128)(2,1)} %get-tuple-element.37.ilo, f32[2,8,8,128,128]{4,3,2,1,0:T(8,128)} %bitcast.23), custom_call_target="tpu_custom_call" | custom-call | tf_op jit(solution)/shard_map/solve_cols/pallas_call | solution.py:313
  411.0 22.2 %finish.1 = f32[8,128,16,128]{3,2,1,0:T(8,128)} custom-call(s32[130]{0:T(256)} %pad_add_fusion.meta, f32[8,16,128,128]{3,2,1,0:T(8,128)} %assemble_8.1.m_ref, bf16[1024,1024]{1,0:T(8,128)(2,1)} %get-tuple-element.39.lhi, bf16[1024,1024]{1,0:T(8,128)(2,1)} %get-tuple-element.40.llo, bf16[1024,2048]{1,0:T(8,128)(2,1)} %get-tuple-element.42.chi, ...), custom_call_target="tpu_custom_call" | custom-call | tf_op jit(solution)/shard_map/finish/pallas_call | solution.py:403
  (32 shorter events, 3.7 us)
Async XLA Ops:
  6.5 389.7 %all-gather.3.cloned.1.call-start = ((), (), s32[]{:S(2)}) async-start(), calls=%async_computation.2 | async-start | bytes 8912896 | tf_op jit(solution)/shard_map/all_gather | solution.py:480
  229.5 4.3 collective-permute-start
  234.7 5.2 %collective-permute-start.1 = (f32[128,128]{1,0:T(8,128)S(1)}, f32[128,128]{1,0:T(8,128)S(1)}, u32[]{:S(2)}, u32[]{:S(2)}) collective-permute-start(f32[128,128]{1,0:T(8,128)S(1)} %broadcast_select_fusion), channel_id=1, source_target_pairs={{0,1},{1,0},{2,3},{3,2},{4,5},{5,4},{6,7},{7,6},{8,9},{9,8},{10,11... | collective-permute-start | bytes 196616 | tf_op jit(solution)/shard_map/ppermute | solution.py:447
  241.0 26.3 %collective-permute-start.8 = (f32[8,128,128]{2,1,0:T(8,128)S(1)}, f32[8,128,128]{2,1,0:T(8,128)S(1)}, u32[]{:S(2)}, u32[]{:S(2)}) collective-permute-start(f32[8,128,128]{2,1,0:T(8,128)S(1)} %slice.16), channel_id=1, source_target_pairs={{0,64},{8,72},{16,80},{24,88},{32,96},{40,104},{48,112},{56,120},{... | collective-permute-start | bytes 1572872 | tf_op jit(solution)/shard_map/ppermute | solution.py:453
  244.2 3.9 collective-permute-start.4
  245.7 5.4 %collective-permute-start.3 = (f32[2,128,128]{2,1,0:T(8,128)S(1)}, f32[2,128,128]{2,1,0:T(8,128)S(1)}, u32[]{:S(2)}, u32[]{:S(2)}) collective-permute-start(f32[2,128,128]{2,1,0:T(8,128)S(1)} %pad_maximum_fusion.3), channel_id=1, source_target_pairs={{0,4},{1,5},{2,6},{3,7},{4,0},{5,1},{6,2},{7,3},{8,12},{9,13},{10,... | collective-permute-start | bytes 393224 | tf_op jit(solution)/shard_map/ppermute | solution.py:447
  246.5 6.0 %collective-permute-start.2 = (f32[2,128,128]{2,1,0:T(8,128)S(1)}, f32[2,128,128]{2,1,0:T(8,128)S(1)}, u32[]{:S(2)}, u32[]{:S(2)}) collective-permute-start(f32[2,128,128]{2,1,0:T(8,128)S(1)} %pad_maximum_fusion.3), channel_id=1, source_target_pairs={{0,2},{1,3},{2,4},{3,5},{4,6},{5,7},{6,0},{7,1},{8,10},{9,11},{10,... | collective-permute-start | bytes 393224 | tf_op jit(solution)/shard_map/ppermute | solution.py:447
  252.5 14.9 %copy-start = (f32[1,16,128,128]{3,2,1,0:T(8,128)S(1)}, f32[1,16,128,128]{3,2,1,0:T(8,128)}, u32[]{:S(2)}) copy-start(f32[1,16,128,128]{3,2,1,0:T(8,128)} %assemble_1.1) | copy-start | bytes 3145732
  252.5 15.7 %collective-permute-start.7 = (f32[4,2,128,128]{3,2,1,0:T(8,128)S(1)}, f32[4,2,128,128]{3,2,1,0:T(8,128)S(1)}, u32[]{:S(2)}, u32[]{:S(2)}) collective-permute-start(f32[4,2,128,128]{3,2,1,0:T(8,128)S(1)} %pad_maximum_fusion.2), channel_id=1, source_target_pairs={{0,48},{8,56},{16,0},{24,8},{32,16},{40,24},{48,32},{56,40},{64,11... | collective-permute-start | bytes 1572872 | tf_op jit(solution)/shard_map/ppermute | solution.py:443
  254.5 13.7 %collective-permute-start.6 = (f32[4,2,128,128]{3,2,1,0:T(8,128)S(1)}, f32[4,2,128,128]{3,2,1,0:T(8,128)S(1)}, u32[]{:S(2)}, u32[]{:S(2)}) collective-permute-start(f32[4,2,128,128]{3,2,1,0:T(8,128)S(1)} %pad_maximum_fusion.2), channel_id=1, source_target_pairs={{0,32},{8,40},{16,48},{24,56},{32,0},{40,8},{48,16},{56,24},{64,96... | collective-permute-start | bytes 1572872 | tf_op jit(solution)/shard_map/ppermute | solution.py:443
  254.5 25.0 %collective-permute-start.5 = (f32[4,2,128,128]{3,2,1,0:T(8,128)S(1)}, f32[4,2,128,128]{3,2,1,0:T(8,128)S(1)}, u32[]{:S(2)}, u32[]{:S(2)}) collective-permute-start(f32[4,2,128,128]{3,2,1,0:T(8,128)S(1)} %pad_maximum_fusion.2), channel_id=1, source_target_pairs={{0,16},{8,24},{16,32},{24,40},{32,48},{40,56},{48,0},{56,8},{64,80... | collective-permute-start | bytes 1572872 | tf_op jit(solution)/shard_map/ppermute | solution.py:443
  279.7 26.5 %copy-start.2 = (f32[4,4,2,128,128]{4,3,2,1,0:T(8,128)}, f32[4,4,2,128,128]{4,3,2,1,0:T(8,128)S(1)}, u32[]{:S(2)}) copy-start(f32[4,4,2,128,128]{4,3,2,1,0:T(8,128)S(1)} %pad_maximum_fusion.own) | copy-start | bytes 6291460
  279.7 24.9 %collective-permute-start.9 = (f32[4,4,2,128,128]{4,3,2,1,0:T(8,128)S(1)}, f32[4,4,2,128,128]{4,3,2,1,0:T(8,128)S(1)}, u32[]{:S(2)}, u32[]{:S(2)}) collective-permute-start(f32[4,4,2,128,128]{4,3,2,1,0:T(8,128)S(1)} %pad_maximum_fusion.own), channel_id=1, source_target_pairs={{0,8},{8,0},{16,24},{24,16},{32,40},{40,32},{48,56},{56,48},{64,72... | collective-permute-start | bytes 6291464 | tf_op jit(solution)/shard_map/ppermute | solution.py:443
  282.7 21.8 %collective-permute-start.10 = (f32[8,128,128]{2,1,0:T(8,128)S(1)}, f32[8,128,128]{2,1,0:T(8,128)S(1)}, u32[]{:S(2)}, u32[]{:S(2)}) collective-permute-start(f32[8,128,128]{2,1,0:T(8,128)S(1)} %get-tuple-element.46), channel_id=1, source_target_pairs={{0,1},{1,0},{2,3},{3,2},{4,5},{5,4},{6,7},{7,6},{8,9},{9,8},{10,11... | collective-permute-start | bytes 1572872 | tf_op jit(solution)/shard_map/ppermute | solution.py:447
  304.7 79.6 %copy-start.1 = (f32[2,8,128,128]{3,2,1,0:T(8,128)}, f32[2,8,128,128]{3,2,1,0:T(8,128)S(1)}, u32[]{:S(2)}) copy-start(f32[2,8,128,128]{3,2,1,0:T(8,128)S(1)} %pad_maximum_fusion.1.refs_0_) | copy-start | bytes 3145732
  304.7 1.4 copy-start.5
  304.7 79.6 %collective-permute-start.13 = (f32[2,8,128,128]{3,2,1,0:T(8,128)S(1)}, f32[2,8,128,128]{3,2,1,0:T(8,128)S(1)}, u32[]{:S(2)}, u32[]{:S(2)}) collective-permute-start(f32[2,8,128,128]{3,2,1,0:T(8,128)S(1)} %pad_maximum_fusion.1.refs_0_), channel_id=1, source_target_pairs={{0,6},{1,7},{2,0},{3,1},{4,2},{5,3},{6,4},{7,5},{8,14},{9,15},{10,... | collective-permute-start | bytes 3145736 | tf_op jit(solution)/shard_map/ppermute | solution.py:447
  306.0 78.2 %collective-permute-start.12 = (f32[2,8,128,128]{3,2,1,0:T(8,128)S(1)}, f32[2,8,128,128]{3,2,1,0:T(8,128)S(1)}, u32[]{:S(2)}, u32[]{:S(2)}) collective-permute-start(f32[2,8,128,128]{3,2,1,0:T(8,128)S(1)} %pad_maximum_fusion.1.refs_0_), channel_id=1, source_target_pairs={{0,4},{1,5},{2,6},{3,7},{4,0},{5,1},{6,2},{7,3},{8,12},{9,13},{10,... | collective-permute-start | bytes 3145736 | tf_op jit(solution)/shard_map/ppermute | solution.py:447
  306.0 78.2 %collective-permute-start.11 = (f32[2,8,128,128]{3,2,1,0:T(8,128)S(1)}, f32[2,8,128,128]{3,2,1,0:T(8,128)}, u32[]{:S(2)}, u32[]{:S(2)}) collective-permute-start(f32[2,8,128,128]{3,2,1,0:T(8,128)S(1)} %pad_maximum_fusion.1.refs_0_), channel_id=1, source_target_pairs={{0,2},{1,3},{2,4},{3,5},{4,6},{5,7},{6,0},{7,1},{8,10},{9,11},{10,... | collective-permute-start | bytes 3145736 | tf_op jit(solution)/shard_map/ppermute | solution.py:447
  384.3 1.0 copy-start.3
  384.3 1.3 copy-start.4
Sparse Core Ops, SparseCore 0:
  279.6 57.7 all-gather.2

commit v3 on v2

--- a/solution.py
+++ b/solution.py
@@ -162,15 +162,63 @@
     )(meta, front, *([landed] * 8))
 
 
+def tile_of_first_col(meta, h):
+    at = jnp.int32(0)
+    found = jnp.int32(0)
+    for kb in range(4):
+        for i in range(2):
+            hit = local_col(meta, h, kb, i) == 0
+            at = jnp.where(hit, 2 * kb + i, at)
+            found = jnp.where(hit, 1, found)
+    return at >> 1, at & 1, found
+
+
+def first_col_kernel(meta, front_ref, *refs):
+    tiles, out_ref = refs[:-1], refs[-1]
+    flat = front_ref.reshape(8 * T * 8, T)
+    for a in range(8):
+        out_ref[a] = flat[pl.ds(a * T * 8, T, stride=8), :]
+    for h in range(2):
+        _, _, found = tile_of_first_col(meta, h)
+
+        @pl.when(found == 1)
+        def _():
+            for ka in range(4):
+                a = local_row(meta, h, ka)
+                out_ref[a] = out_ref[a] + tiles[4 * h + ka][...]
+
+
+def first_col(meta, front, landed):
+    def tile_spec(h, ka):
+        def at(i, m):
+            kb, j, _ = tile_of_first_col(m, h)
+            return source_col(m, h, kb), h, ka, j, 0, 0
+
+        return pl.BlockSpec((None, None, None, None, T, T), at)
+
+    whole = pl.BlockSpec((8, T, T), lambda i, m: (0, 0, 0))
+    return pl.pallas_call(
+        first_col_kernel,
+        grid_spec=pltpu.PrefetchScalarGridSpec(
+            num_scalar_prefetch=1,
+            grid=(1,),
+            in_specs=[pl.BlockSpec((8, T, 8, T), lambda i, m: (0, 0, 0, 0))]
+            + [tile_spec(h, ka) for h in range(2) for ka in range(4)],
+            out_specs=whole,
+        ),
+        out_shape=jax.ShapeDtypeStruct((8, T, T), F32),
+        compiler_params=params(),
+        name="first_col",
+    )(meta, front, *([landed] * 8))
+
+
 def root(x):
     r = lax.rsqrt(x)
     return r * (1.5 - 0.5 * x * r * r)
 
 
 def inverse_of(x):
-    r = pl.reciprocal(x, approx=True)
-    r = r * (2.0 - x * r)
-    return r * (2.0 - x * r)
+    return pl.reciprocal(x, approx=False)
 
 
 def invert_kernel(meta, own, other, hi_ref, lo_ref, a_ref, t_ref, l_ref):
@@ -294,43 +342,16 @@
 
 
 B = 256
-
-
-def solve_cols_kernel(ihi, ilo, x_ref, ohi, olo, y_ref):
-    for k in range(W // B):
-        x = jnp.concatenate(
-            [jnp.concatenate([x_ref[q, 0], x_ref[q, 1]], axis=1) for q in (2 * k, 2 * k + 1)], axis=0
-        )
-        cols = slice(k * B, (k + 1) * B)
-        y = dot3((ihi[k * B :, cols], ilo[k * B :, cols]), split(x))
-        y_ref[k * B :, :] = y if k == 0 else y_ref[k * B :, :] + y
-        ohi[cols, :], olo[cols, :] = split(y_ref[cols, :])
-
-
-def solve_cols(inverse, x):
-    whole = pl.BlockSpec((W, W), lambda i: (0, 0))
-    out = pl.BlockSpec((W, B), lambda i: (0, i))
-    return pl.pallas_call(
-        solve_cols_kernel,
-        grid=(8,),
-        in_specs=[
-            whole,
-            whole,
-            pl.BlockSpec((None, 8, 2, T, T), lambda i: (i // 4, 0, i % 4, 0, 0)),
-        ],
-        out_specs=[out, out],
-        out_shape=[jax.ShapeDtypeStruct((W, 2048), BF16)] * 2,
-        scratch_shapes=[pltpu.VMEM((W, B), F32)],
-        compiler_params=params(),
-        name="solve_cols",
-    )(*inverse, x)
-
-
 H = 4
-
-
-def solve_rows_kernel(meta, ihi, ilo, *refs):
-    xs, (ohi, olo, pan, xhi, xlo, y_ref) = refs[:4], refs[4:]
+F = 2
+ROW_STEPS = 8 // H
+COL_STEPS = 2048 // B
+END_STEPS = 8 // F
+
+
+def rows_step(meta, i, inverse, xs, lhs, pan, x_refs, y_ref):
+    ihi, ilo = inverse
+    xhi, xlo = x_refs
     for d in range(8):
         q = (((meta[COL_AT] >> 1) - (d >> 1)) & 3) * 2 + ((meta[COL_AT] ^ d) & 1)
         cols = pl.ds(pl.multiple_of(q * T, T), T)
@@ -343,46 +364,36 @@
         y_ref[:, rows] = dot3((xhi[:, :n], xlo[:, :n]), (ihi[rows, :n], ilo[rows, :n]), NT)
     at = pl.multiple_of(meta[COL_AT] * T, T)
     for a in range(H):
-        pan[a] = y_ref[a * T : (a + 1) * T, pl.ds(at, T)]
+        pan[i * H + a] = y_ref[a * T : (a + 1) * T, pl.ds(at, T)]
     row = meta[ROW_AT]
     limit = jnp.where(row < 4, 0, jnp.where(row < 8, 512, W))
-    limit = jnp.where(pl.program_id(0) == 0, limit, W)
+    limit = jnp.where(i == 0, limit, W)
     inside = lax.broadcasted_iota(jnp.int32, (T, W), 1) < limit
     y_ref[:T, :] = jnp.where(inside, y_ref[:T, :], F32(0))
-    ohi[...], olo[...] = split(y_ref[...])
-
-
-def solve_rows(meta, inverse, xs):
-    whole = pl.BlockSpec((W, W), lambda i, m: (0, 0))
-    out = pl.BlockSpec((H * T, W), lambda i, m: (i, 0))
-    tiles = pl.BlockSpec((H, T, T), lambda i, m: (i, 0, 0))
-    return pl.pallas_call(
-        solve_rows_kernel,
-        grid_spec=pltpu.PrefetchScalarGridSpec(
-            num_scalar_prefetch=1,
-            grid=(8 // H,),
-            in_specs=[whole, whole] + [pl.BlockSpec((2, H, T, T), lambda i, m: (0, i, 0, 0))] * 4,
-            out_specs=[out, out, tiles],
-            scratch_shapes=[
-                pltpu.VMEM((H * T, W), BF16),
-                pltpu.VMEM((H * T, W), BF16),
-                pltpu.VMEM((H * T, W), F32),
-            ],
-        ),
-        out_shape=[jax.ShapeDtypeStruct((W, W), BF16)] * 2 + [jax.ShapeDtypeStruct((8, T, T), F32)],
-        compiler_params=params(),
-        name="solve_rows",
-    )(meta, *inverse, *xs)
-
-
-F = 2
-
-
-def finish_kernel(meta, m_ref, lhi, llo, chi, clo, pan, out):
+    where = pl.ds(pl.multiple_of(i * H * T, H * T), H * T)
+    lhs[0][where, :], lhs[1][where, :] = split(y_ref[...])
+
+
+def cols_step(i, inverse, x_ref, rhs, y_ref):
+    ihi, ilo = inverse
+    where = pl.ds(pl.multiple_of(i * B, B), B)
+    for k in range(W // B):
+        x = jnp.concatenate(
+            [jnp.concatenate([x_ref[q, 0], x_ref[q, 1]], axis=1) for q in (2 * k, 2 * k + 1)], axis=0
+        )
+        cols = slice(k * B, (k + 1) * B)
+        y = dot3((ihi[k * B :, cols], ilo[k * B :, cols]), split(x))
+        y_ref[k * B :, :] = y if k == 0 else y_ref[k * B :, :] + y
+        rhs[0][cols, where], rhs[1][cols, where] = split(y_ref[cols, :])
+
+
+def end_step(meta, i, m_ref, lhs, rhs, pan, out):
     flat = out.reshape(F * T * 16, T)
+    where = pl.ds(pl.multiple_of(i * F * T, F * T), F * T)
+    left = lhs[0][where, :], lhs[1][where, :]
     for n in range(0, 2048, 512):
         cols = slice(n, n + 512)
-        p = dot3((lhi[...], llo[...]), (chi[:, cols], clo[:, cols]))
+        p = dot3(left, (rhs[0][:, cols], rhs[1][:, cols]))
         for a in range(F):
             for at in range(n // T, n // T + 4):
                 lc = (at % 8) * 2 + at // 8
@@ -390,35 +401,67 @@
                     m_ref[a, at] - p[a * T : (a + 1) * T, (at * T) % 512 : (at * T) % 512 + T]
                 )
     for a in range(F):
-        kept = (pl.program_id(0) * F + a == 0) & (meta[ROW_AT] < 4) & (meta[COL_AT] >= 4)
+        kept = (i * F + a == 0) & (meta[ROW_AT] < 4) & (meta[COL_AT] >= 4)
 
         @pl.when(jnp.logical_not(kept))
         def _():
-            flat[pl.ds(a * T * 16, T, stride=16), :] = pan[a]
-
-
-def finish(meta, m, rows, cols, pan):
-    whole = pl.BlockSpec((W, 2048), lambda i, m: (0, 0))
-    lhs = pl.BlockSpec((F * T, W), lambda i, m: (i, 0))
+            flat[pl.ds(a * T * 16, T, stride=16), :] = pan[i * F + a]
+
+
+def finish_kernel(meta, ihi, ilo, x0, x1, x2, x3, xc, m_ref, out, lhi, llo, chi, clo, pan, xhi, xlo, yr, yc):
+    i = pl.program_id(0)
+
+    @pl.when(i < ROW_STEPS)
+    def _():
+        rows_step(meta, i, (ihi, ilo), (x0, x1, x2, x3), (lhi, llo), pan, (xhi, xlo), yr)
+
+    @pl.when((i >= ROW_STEPS) & (i < ROW_STEPS + COL_STEPS))
+    def _():
+        cols_step(i - ROW_STEPS, (ihi, ilo), xc, (chi, clo), yc)
+
+    @pl.when(i >= ROW_STEPS + COL_STEPS)
+    def _():
+        end_step(meta, i - ROW_STEPS - COL_STEPS, m_ref, (lhi, llo), (chi, clo), pan, out)
+
+
+def finish(meta, inverse, rows_x, cols_x, m):
+    def part(i, before, count):
+        return jnp.clip(i - before, 0, count - 1)
+
+    def col_block(i, m):
+        j = part(i, ROW_STEPS, COL_STEPS)
+        return j // 4, 0, j % 4, 0, 0
+
+    def end_block(i, m):
+        return part(i, ROW_STEPS + COL_STEPS, END_STEPS), 0, 0, 0
+
+    whole = pl.BlockSpec((W, W), lambda i, m: (0, 0), pipeline_mode=pl.Buffered(1))
+    tiles = pl.BlockSpec((2, H, T, T), lambda i, m: (0, part(i, 0, ROW_STEPS), 0, 0))
     return pl.pallas_call(
         finish_kernel,
         grid_spec=pltpu.PrefetchScalarGridSpec(
             num_scalar_prefetch=1,
-            grid=(8 // F,),
-            in_specs=[
-                pl.BlockSpec((F, 16, T, T), lambda i, m: (i, 0, 0, 0)),
-                lhs,
-                lhs,
-                whole,
-                whole,
-                pl.BlockSpec((F, T, T), lambda i, m: (i, 0, 0)),
+            grid=(ROW_STEPS + COL_STEPS + END_STEPS,),
+            in_specs=[whole, whole]
+            + [tiles] * 4
+            + [pl.BlockSpec((None, 8, 2, T, T), col_block), pl.BlockSpec((F, 16, T, T), end_block)],
+            out_specs=pl.BlockSpec((F, T, 16, T), end_block),
+            scratch_shapes=[
+                pltpu.VMEM((W, W), BF16),
+                pltpu.VMEM((W, W), BF16),
+                pltpu.VMEM((W, 2048), BF16),
+                pltpu.VMEM((W, 2048), BF16),
+                pltpu.VMEM((8, T, T), F32),
+                pltpu.VMEM((H * T, W), BF16),
+                pltpu.VMEM((H * T, W), BF16),
+                pltpu.VMEM((H * T, W), F32),
+                pltpu.VMEM((W, B), F32),
             ],
-            out_specs=pl.BlockSpec((F, T, 16, T), lambda i, m: (i, 0, 0, 0)),
         ),
         out_shape=jax.ShapeDtypeStruct((8, T, 16, T), F32),
         compiler_params=params(),
         name="finish",
-    )(meta, m, *rows, *cols, pan)
+    )(meta, *inverse, *rows_x, cols_x, m)
 
 
 def exchange(x, axis):
@@ -465,26 +508,24 @@
 
     tile = jnp.where(upper, first[0], down(first[0]))
     two = jnp.stack([tile, along_col(tile, 0, 1)])
-    two, first = lax.optimization_barrier((two, first))
+    two, first, landed, front = lax.optimization_barrier((two, first, landed, front))
     line = jnp.stack([two] + [along_col(two, dx, 0) for dx in (1, 2, 3)])
     ours = jnp.where(upper, first[:8], down(first[8:]))
-    line, landed, front = lax.optimization_barrier((line, landed, front))
+    mine = first_col(meta, front, landed)
+    line, mine, landed, front = lax.optimization_barrier((line, mine, landed, front))
     parts = [line] + [along_row(line, 0, dz, 0) for dz in (1, 2, 3)]
+    pair = jnp.stack([mine, along_col(mine, 0, 1)])
     matrix = assemble(meta, front, landed, 0, 8)
-    parts, matrix, ours = lax.optimization_barrier((parts, matrix, ours))
+    parts, pair, ours, matrix = lax.optimization_barrier((parts, pair, ours, matrix))
     own = jnp.stack(parts)
     other = along_row(own, 0, 0, 1)
 
-    mine = matrix[:, 0]
-    pair = jnp.stack([mine, along_col(mine, 0, 1)])
     cols_x = lax.all_gather(ours, "row").reshape(2, 8, 8, T, T)
     other, pair = lax.optimization_barrier((other, pair))
     rows_x = [pair] + [along_col(pair, dx, 0) for dx in (1, 2, 3)]
 
     inverse = invert(meta, own, other)
-    *rows_l, pan = solve_rows(meta, inverse, rows_x)
-    cols_l = solve_cols(inverse, cols_x)
-    return finish(meta, matrix, rows_l, cols_l, pan)
+    return finish(meta, inverse, rows_x, cols_x, matrix)
 
 
 def solution(mesh):

time: 445 us -> 410 us (0.921)
  waiting for transfers between devices: 39.8 us -> 20 us
  Pallas kernels: 156 us -> 144 us
    ppermute x8, waiting for transfers between devices: 27.2 us -> 3.54 us  [along_col(): lax.ppermute(v, 'col', [(col_id(x, y), col_id(x + dx, y + dy)) for x in r...]
    pallas_call x2 -> x1, Pallas kernels: 25.4 us -> 4.07 us  [first_col(): pl.pallas_call(first_col_kernel, grid_spec=pltpu.PrefetchScalarGridSpec(n...]
    pallas_call x1, Pallas kernels: 22.2 us -> 37.8 us  [finish(): pl.pallas_call(finish_kernel, grid_spec=pltpu.PrefetchScalarGridSpec(num_...]
    pallas_call x1, Pallas kernels: 78 us -> 71.4 us  [invert(): pl.pallas_call(invert_kernel, in_specs=[pl.BlockSpec(memory_space=pltpu.S...]
  transfers between devices with their start and end apart: 15 -> 15, of which waited for: 7 -> 5; matrix products, arithmetic and copies ran while one was open for 1% -> 1% of each run, Pallas kernels for 23% -> 21%
where the time goes in v3:
time: 410 us; the launch traced here: 409 us
  blocking collectives  202 us (49%)
  Pallas kernels  144 us (35%)
  starting transfers between devices  21.8 us (5%)
  waiting for transfers between devices  20 us (5%)
  between operations  13.5 us (3%)
    all_to_all x2, blocking collectives, exchange(): return lax.all_to_all(x, axis, split_axis=0, concat_axis=0, tiled=True)  202 us
    pallas_call x1, Pallas kernels, invert(): pl.pallas_call(invert_kernel, in_specs=[pl.BlockSpec(memory_space=pltpu.S...  71.4 us
    pallas_call x1, Pallas kernels, finish(): pl.pallas_call(finish_kernel, grid_spec=pltpu.PrefetchScalarGridSpec(num_...  37.8 us
    pallas_call x2, Pallas kernels, assemble(): pl.pallas_call(functools.partial(assemble_kernel, start), grid_spec=pltpu...  15.8 us
    ppermute x4, waiting for transfers between devices, along_row(): return lax.ppermute(v, 'row', pairs)  15.1 us
    ppermute x8, starting transfers between devices, along_col(): lax.ppermute(v, 'col', [(col_id(x, y), col_id(x + dx, y + dy)) for x in r...  11.2 us
  transfers between devices with their start and end apart: 15, of which 5 were waited for; matrix products, arithmetic and copies ran while one was open for 1% of the time, Pallas kernels for 21%

profile of v3, /device:TPU:1, one launch (start us, length us, event | category | flops | bytes accessed | tf_op | source)
XLA Modules:
  0.0 409.5 jit_solution(9795939307325277298)
XLA Ops:
  6.5 0.8 reshape.8
  8.0 7.5 %pack_rows.1 = f32[16,8,128,128]{3,2,1,0:T(8,128)} custom-call(s32[130]{0:T(256)} %pad_add_fusion.meta, f32[2,4,128,8,128]{4,3,2,1,0:T(8,128)} %child_ref.1), custom_call_target="tpu_custom_call" | custom-call | tf_op jit(solution)/shard_map/pack_rows/pallas_call | solution.py:81
  15.5 102.0 %all_to_all.10.refs_0_.refs_1_.refs_2_.refs_3_ = f32[16,8,128,128]{3,2,1,0:T(8,128)} all-to-all(f32[16,8,128,128]{3,2,1,0:T(8,128)} %pack_rows.1), channel_id=1, replica_groups=mesh['row'=16,'col'=8] {'row'}, dimensions={0} | all-to-all | bytes 16777216 | tf_op jit(solution)/shard_map/all_to_all | solution.py:468
  117.5 7.3 %pack_cols.1 = f32[8,2,4,2,128,128]{5,4,3,2,1,0:T(8,128)} custom-call(s32[130]{0:T(256)} %pad_add_fusion.meta, f32[16,8,128,128]{3,2,1,0:T(8,128)} %all_to_all.10.refs_0_.refs_1_.refs_2_.refs_3_, f32[16,8,128,128]{3,2,1,0:T(8,128)} %all_to_all.10.refs_0_.refs_1_.refs_2_.refs_3_, f32[16,8,128,128]{3,2,1,0:T(8,128)} %all_to_all.10.refs_0_.refs_1_.refs_2_.refs_3_, ...), custom_call_target="tpu_custom_call" | custom-call | tf_op jit(solution)/shard_map/pack_cols/pallas_call | solution.py:106
  124.8 100.2 %all_to_all.11.refs_0_.refs_1_.refs_2_.refs_3_.refs_4_.refs_5_.refs_6_.refs_7_ = f32[8,2,4,2,128,128]{5,4,3,2,1,0:T(8,128)} all-to-all(f32[8,2,4,2,128,128]{5,4,3,2,1,0:T(8,128)} %pack_cols.1), channel_id=1, replica_groups=mesh['row'=16,'col'=8] {'col'}, dimensions={0} | all-to-all | bytes 16777216 | tf_op jit(solution)/shard_map/all_to_all | solution.py:468
  225.1 3.6 assemble_1.1
  228.7 0.8 slice_bitcast_fusion
  229.5 3.0 collective-permute-start
  232.6 1.3 collective-permute-done
  233.9 0.8 broadcast_select_fusion
  234.7 2.8 collective-permute-start.1
  237.5 2.4 collective-permute-done.1
  239.9 1.1 slice.13
  241.0 3.2 collective-permute-start.9
  244.2 1.5 collective-permute-start.4
  245.8 0.7 collective-permute-start.3
  246.5 0.8 collective-permute-start.2
  247.3 4.1 first_col.1
  251.3 1.1 collective-permute-done.2
  252.5 2.2 collective-permute-start.8
  254.8 2.0 collective-permute-start.7
  257.3 12.1 %assemble_8.1.m_ref = f32[8,16,128,128]{3,2,1,0:T(8,128)} custom-call(s32[130]{0:T(256)} %pad_add_fusion.meta, f32[8,128,16,128]{3,2,1,0:T(8,128)} %front_ref.3, f32[8,2,4,2,128,128]{5,4,3,2,1,0:T(8,128)} %all_to_all.11.refs_0_.refs_1_.refs_2_.refs_3_.refs_4_.refs_5_.refs_6_.refs_7_, ...), custom_call_target="tpu_custom_call" | custom-call | bytes 20971520 | tf_op jit(solution)/shard_map/assemble_8/pallas_call | solution.py:149
  269.5 0.9 slice_select_fusion
  270.5 11.3 %collective-permute-done.5 = f32[4,2,128,128]{3,2,1,0:T(8,128)} collective-permute-done((f32[4,2,128,128]{3,2,1,0:T(8,128)S(1)}, f32[4,2,128,128]{3,2,1,0:T(8,128)}, u32[]{:S(2)}, u32[]{:S(2)}) %collective-permute-start.5) | collective-permute-done | bytes 524320 | tf_op jit(solution)/shard_map/ppermute | solution.py:486
  281.9 1.4 pad_maximum_fusion.own
  283.3 1.8 collective-permute-start.10
  285.1 3.8 collective-permute-done.10.other
  288.9 1.3 collective-permute-start.13
  290.2 1.5 collective-permute-start.12
  292.1 71.4 %invert.1 = (bf16[1024,1024]{1,0:T(8,128)(2,1)}, bf16[1024,1024]{1,0:T(8,128)(2,1)}) custom-call(s32[130]{0:T(256)} %pad_add_fusion.meta, f32[4,4,2,128,128]{4,3,2,1,0:T(8,128)} %copy-done.3, f32[4,4,2,128,128]{4,3,2,1,0:T(8,128)} %copy-done.6), custom_call_target="tpu_custom_call" | custom-call | flops 80000000000 | bytes 8388608 | tf_op jit(solution)/shard_map/invert/pallas_call | solution.py:328
  363.6 0.9 copy-done.4
  364.8 37.8 %finish.1 = f32[8,128,16,128]{3,2,1,0:T(8,128)} custom-call(s32[130]{0:T(256)} %pad_add_fusion.meta, bf16[1024,1024]{1,0:T(8,128)(2,1)} %get-tuple-element.38.ihi, bf16[1024,1024]{1,0:T(8,128)(2,1)} %get-tuple-element.39.ilo, f32[2,8,128,128]{3,2,1,0:T(8,128)} %copy-done.1, f32[2,8,128,128]{3,2,1,0:T(8,128)} %collective-permute-done.11.x1, ...), custom_call_target="tpu_custom_call" | custom-call | tf_op jit(solution)/shard_map/finish/pallas_call | solution.py:440
  (32 shorter events, 2.2 us)
Async XLA Ops:
  6.5 357.0 %all-gather.3.cloned.1.call-start = ((), (), s32[]{:S(2)}) async-start(), calls=%async_computation.2 | async-start | bytes 8912896 | tf_op jit(solution)/shard_map/all_gather | solution.py:523
  229.5 4.3 %collective-permute-start = (f32[128,128]{1,0:T(8,128)S(1)}, f32[128,128]{1,0:T(8,128)S(1)}, u32[]{:S(2)}, u32[]{:S(2)}) collective-permute-start(f32[128,128]{1,0:T(8,128)S(1)} %slice_bitcast_fusion), channel_id=1, source_target_pairs={{0,64},{8,72},{16,80},{24,88},{32,96},{40,104},{48,112},{56,120},{... | collective-permute-start | bytes 196616 | tf_op jit(solution)/shard_map/ppermute | solution.py:496
  234.7 5.2 %collective-permute-start.1 = (f32[128,128]{1,0:T(8,128)S(1)}, f32[128,128]{1,0:T(8,128)S(1)}, u32[]{:S(2)}, u32[]{:S(2)}) collective-permute-start(f32[128,128]{1,0:T(8,128)S(1)} %broadcast_select_fusion), channel_id=1, source_target_pairs={{0,1},{1,0},{2,3},{3,2},{4,5},{5,4},{6,7},{7,6},{8,9},{9,8},{10,11... | collective-permute-start | bytes 196616 | tf_op jit(solution)/shard_map/ppermute | solution.py:490
  241.0 28.4 %collective-permute-start.9 = (f32[8,128,128]{2,1,0:T(8,128)S(1)}, f32[8,128,128]{2,1,0:T(8,128)S(1)}, u32[]{:S(2)}, u32[]{:S(2)}) collective-permute-start(f32[8,128,128]{2,1,0:T(8,128)S(1)} %slice.13), channel_id=1, source_target_pairs={{0,64},{8,72},{16,80},{24,88},{32,96},{40,104},{48,112},{56,120},{... | collective-permute-start | bytes 1572872 | tf_op jit(solution)/shard_map/ppermute | solution.py:496
  244.2 7.1 %collective-permute-start.4 = (f32[2,128,128]{2,1,0:T(8,128)S(1)}, f32[2,128,128]{2,1,0:T(8,128)S(1)}, u32[]{:S(2)}, u32[]{:S(2)}) collective-permute-start(f32[2,128,128]{2,1,0:T(8,128)S(1)} %pad_maximum_fusion.3), channel_id=1, source_target_pairs={{0,6},{1,7},{2,0},{3,1},{4,2},{5,3},{6,4},{7,5},{8,14},{9,15},{10,... | collective-permute-start | bytes 393224 | tf_op jit(solution)/shard_map/ppermute | solution.py:490
  245.8 5.6 %collective-permute-start.3 = (f32[2,128,128]{2,1,0:T(8,128)S(1)}, f32[2,128,128]{2,1,0:T(8,128)S(1)}, u32[]{:S(2)}, u32[]{:S(2)}) collective-permute-start(f32[2,128,128]{2,1,0:T(8,128)S(1)} %pad_maximum_fusion.3), channel_id=1, source_target_pairs={{0,4},{1,5},{2,6},{3,7},{4,0},{5,1},{6,2},{7,3},{8,12},{9,13},{10,... | collective-permute-start | bytes 393224 | tf_op jit(solution)/shard_map/ppermute | solution.py:490
  246.5 6.0 %collective-permute-start.2 = (f32[2,128,128]{2,1,0:T(8,128)S(1)}, f32[2,128,128]{2,1,0:T(8,128)S(1)}, u32[]{:S(2)}, u32[]{:S(2)}) collective-permute-start(f32[2,128,128]{2,1,0:T(8,128)S(1)} %pad_maximum_fusion.3), channel_id=1, source_target_pairs={{0,2},{1,3},{2,4},{3,5},{4,6},{5,7},{6,0},{7,1},{8,10},{9,11},{10,... | collective-permute-start | bytes 393224 | tf_op jit(solution)/shard_map/ppermute | solution.py:490
  252.5 16.9 %copy-start = (f32[1,16,128,128]{3,2,1,0:T(8,128)S(1)}, f32[1,16,128,128]{3,2,1,0:T(8,128)}, u32[]{:S(2)}) copy-start(f32[1,16,128,128]{3,2,1,0:T(8,128)} %assemble_1.1) | copy-start | bytes 3145732
  252.5 17.9 %copy-start.2 = (f32[8,128,128]{2,1,0:T(8,128)S(1)}, f32[8,128,128]{2,1,0:T(8,128)}, u32[]{:S(2)}) copy-start(f32[8,128,128]{2,1,0:T(8,128)} %first_col.1) | copy-start | bytes 1572868
  252.5 17.9 %collective-permute-start.8 = (f32[8,128,128]{2,1,0:T(8,128)}, f32[8,128,128]{2,1,0:T(8,128)S(1)}, u32[]{:S(2)}, u32[]{:S(2)}) collective-permute-start(f32[8,128,128]{2,1,0:T(8,128)} %first_col.1), channel_id=1, source_target_pairs={{0,1},{1,0},{2,3},{3,2},{4,5},{5,4},{6,7},{7,6},{8,9},{9,8},{10,11... | collective-permute-start | bytes 1572872 | tf_op jit(solution)/shard_map/ppermute | solution.py:490
  254.8 15.8 %collective-permute-start.7 = (f32[4,2,128,128]{3,2,1,0:T(8,128)S(1)}, f32[4,2,128,128]{3,2,1,0:T(8,128)S(1)}, u32[]{:S(2)}, u32[]{:S(2)}) collective-permute-start(f32[4,2,128,128]{3,2,1,0:T(8,128)S(1)} %pad_maximum_fusion.2), channel_id=1, source_target_pairs={{0,48},{8,56},{16,0},{24,8},{32,16},{40,24},{48,32},{56,40},{64,11... | collective-permute-start | bytes 1572872 | tf_op jit(solution)/shard_map/ppermute | solution.py:486
  256.7 13.8 %collective-permute-start.6 = (f32[4,2,128,128]{3,2,1,0:T(8,128)S(1)}, f32[4,2,128,128]{3,2,1,0:T(8,128)}, u32[]{:S(2)}, u32[]{:S(2)}) collective-permute-start(f32[4,2,128,128]{3,2,1,0:T(8,128)S(1)} %pad_maximum_fusion.2), channel_id=1, source_target_pairs={{0,32},{8,40},{16,48},{24,56},{32,0},{40,8},{48,16},{56,24},{64,96... | collective-permute-start | bytes 1572872 | tf_op jit(solution)/shard_map/ppermute | solution.py:486
  256.7 25.1 %collective-permute-start.5 = (f32[4,2,128,128]{3,2,1,0:T(8,128)S(1)}, f32[4,2,128,128]{3,2,1,0:T(8,128)}, u32[]{:S(2)}, u32[]{:S(2)}) collective-permute-start(f32[4,2,128,128]{3,2,1,0:T(8,128)S(1)} %pad_maximum_fusion.2), channel_id=1, source_target_pairs={{0,16},{8,24},{16,32},{24,40},{32,48},{40,56},{48,0},{56,8},{64,80... | collective-permute-start | bytes 1572872 | tf_op jit(solution)/shard_map/ppermute | solution.py:486
  270.5 21.3 %copy-start.1 = (f32[2,8,128,128]{3,2,1,0:T(8,128)}, f32[2,8,128,128]{3,2,1,0:T(8,128)S(1)}, u32[]{:S(2)}) copy-start(f32[2,8,128,128]{3,2,1,0:T(8,128)S(1)} %pad_maximum_fusion.1.x0) | copy-start | bytes 3145732
  283.3 8.8 %copy-start.3 = (f32[4,4,2,128,128]{4,3,2,1,0:T(8,128)}, f32[4,4,2,128,128]{4,3,2,1,0:T(8,128)S(1)}, u32[]{:S(2)}) copy-start(f32[4,4,2,128,128]{4,3,2,1,0:T(8,128)S(1)} %pad_maximum_fusion.own) | copy-start | bytes 6291460
  283.3 5.6 %collective-permute-start.10 = (f32[4,4,2,128,128]{4,3,2,1,0:T(8,128)S(1)}, f32[4,4,2,128,128]{4,3,2,1,0:T(8,128)S(1)}, u32[]{:S(2)}, u32[]{:S(2)}) collective-permute-start(f32[4,4,2,128,128]{4,3,2,1,0:T(8,128)S(1)} %pad_maximum_fusion.own), channel_id=1, source_target_pairs={{0,8},{8,0},{16,24},{24,16},{32,40},{40,32},{48,56},{56,48},{64,72... | collective-permute-start | bytes 6291464 | tf_op jit(solution)/shard_map/ppermute | solution.py:486
  288.9 1.3 copy-start.6
  288.9 74.6 %collective-permute-start.13 = (f32[2,8,128,128]{3,2,1,0:T(8,128)S(1)}, f32[2,8,128,128]{3,2,1,0:T(8,128)S(1)}, u32[]{:S(2)}, u32[]{:S(2)}) collective-permute-start(f32[2,8,128,128]{3,2,1,0:T(8,128)S(1)} %pad_maximum_fusion.1.x0), channel_id=1, source_target_pairs={{0,6},{1,7},{2,0},{3,1},{4,2},{5,3},{6,4},{7,5},{8,14},{9,15},{10,... | collective-permute-start | bytes 3145736 | tf_op jit(solution)/shard_map/ppermute | solution.py:490
  290.2 73.3 %collective-permute-start.12 = (f32[2,8,128,128]{3,2,1,0:T(8,128)S(1)}, f32[2,8,128,128]{3,2,1,0:T(8,128)S(1)}, u32[]{:S(2)}, u32[]{:S(2)}) collective-permute-start(f32[2,8,128,128]{3,2,1,0:T(8,128)S(1)} %pad_maximum_fusion.1.x0), channel_id=1, source_target_pairs={{0,4},{1,5},{2,6},{3,7},{4,0},{5,1},{6,2},{7,3},{8,12},{9,13},{10,... | collective-permute-start | bytes 3145736 | tf_op jit(solution)/shard_map/ppermute | solution.py:490
  291.8 71.7 %collective-permute-start.11 = (f32[2,8,128,128]{3,2,1,0:T(8,128)S(1)}, f32[2,8,128,128]{3,2,1,0:T(8,128)}, u32[]{:S(2)}, u32[]{:S(2)}) collective-permute-start(f32[2,8,128,128]{3,2,1,0:T(8,128)S(1)} %pad_maximum_fusion.1.x0), channel_id=1, source_target_pairs={{0,2},{1,3},{2,4},{3,5},{4,6},{5,7},{6,0},{7,1},{8,10},{9,11},{10,... | collective-permute-start | bytes 3145736 | tf_op jit(solution)/shard_map/ppermute | solution.py:490
  363.5 1.0 copy-start.4
  363.5 1.3 copy-start.5
Sparse Core Ops, SparseCore 0:
  282.0 49.1 all-gather.2

commit v4 on v3

--- a/solution.py
+++ b/solution.py
@@ -71,52 +71,88 @@
     return dot(a[0], b[0], dims) + (dot(a[0], b[1], dims) + dot(a[1], b[0], dims))
 
 
-def pack_rows_kernel(meta, child_ref, out_ref):
-    flat = child_ref.reshape(T * 8, T)
-    for j in range(8):
-        out_ref[0, j] = flat[pl.ds(j, T, stride=8), :]
+def pack_rows_kernel(meta, child, out, held, packed, in_sems, out_sems):
+    blocks = [(h, k) for h in range(2) for k in range(4)]
+    loads = [
+        pltpu.make_async_copy(child.at[h, k], held.at[n], in_sems.at[n]) for n, (h, k) in enumerate(blocks)
+    ]
+    stores = [
+        pltpu.make_async_copy(
+            packed.at[n], out.at[(meta[ROW_AT] + shift(meta, h, k)) & 15], out_sems.at[n]
+        )
+        for n, (h, k) in enumerate(blocks)
+    ]
+    for load in loads:
+        load.start()
+    flat = held.reshape(8 * T * 8, T)
+    for n in range(8):
+        loads[n].wait()
+        for j in range(8):
+            packed[n, j] = flat[pl.ds(n * T * 8 + j, T, stride=8), :]
+        stores[n].start()
+    for store in stores:
+        store.wait()
 
 
 def pack_rows(meta, child):
     return pl.pallas_call(
         pack_rows_kernel,
-        grid_spec=pltpu.PrefetchScalarGridSpec(
-            num_scalar_prefetch=1,
-            grid=(2, 4),
-            in_specs=[pl.BlockSpec((None, None, T, 8, T), lambda h, k, m: (h, k, 0, 0, 0))],
-            out_specs=pl.BlockSpec(
-                (1, 8, T, T), lambda h, k, m: ((m[ROW_AT] + shift(m, h, k)) & 15, 0, 0, 0)
-            ),
-        ),
+        in_specs=[pl.BlockSpec(memory_space=pltpu.SMEM), pl.BlockSpec(memory_space=pl.ANY)],
+        out_specs=pl.BlockSpec(memory_space=pl.ANY),
         out_shape=jax.ShapeDtypeStruct((16, 8, T, T), F32),
+        scratch_shapes=[
+            pltpu.VMEM((8, T, 8, T), F32),
+            pltpu.VMEM((8, 8, T, T), F32),
+            pltpu.SemaphoreType.DMA((8,)),
+            pltpu.SemaphoreType.DMA((8,)),
+        ],
         compiler_params=params(),
         name="pack_rows",
     )(meta, child)
 
 
-def pack_cols_kernel(meta, *refs):
-    for lev in range(4):
-        refs[4][lev] = refs[lev][...]
+def pack_cols_kernel(meta, arrived, out, held, in_sems, out_sems):
+    pairs = [(h, kb) for h in range(2) for kb in range(4)]
+    loads = [
+        [
+            pltpu.make_async_copy(
+                arrived.at[source_row(meta, h, lev), pl.ds(2 * kb, 2)],
+                held.at[n, lev],
+                in_sems.at[n, lev],
+            )
+            for lev in range(4)
+        ]
+        for n, (h, kb) in enumerate(pairs)
+    ]
+    stores = [
+        pltpu.make_async_copy(held.at[n], out.at[dest_col(meta, h, kb), h], out_sems.at[n])
+        for n, (h, kb) in enumerate(pairs)
+    ]
+    for group in loads:
+        for load in group:
+            load.start()
+    for n in range(8):
+        for load in loads[n]:
+            load.wait()
+        stores[n].start()
+    for store in stores:
+        store.wait()
 
 
 def pack_cols(meta, arrived):
-    def source(lev):
-        return pl.BlockSpec((None, 2, T, T), lambda h, kb, m: (source_row(m, h, lev), kb, 0, 0))
-
     return pl.pallas_call(
         pack_cols_kernel,
-        grid_spec=pltpu.PrefetchScalarGridSpec(
-            num_scalar_prefetch=1,
-            grid=(2, 4),
-            in_specs=[source(lev) for lev in range(4)],
-            out_specs=pl.BlockSpec(
-                (None, None, 4, 2, T, T), lambda h, kb, m: (dest_col(m, h, kb), h, 0, 0, 0, 0)
-            ),
-        ),
+        in_specs=[pl.BlockSpec(memory_space=pltpu.SMEM), pl.BlockSpec(memory_space=pl.ANY)],
+        out_specs=pl.BlockSpec(memory_space=pl.ANY),
         out_shape=jax.ShapeDtypeStruct((8, 2, 4, 2, T, T), F32),
+        scratch_shapes=[
+            pltpu.VMEM((8, 4, 2, T, T), F32),
+            pltpu.SemaphoreType.DMA((8, 4)),
+            pltpu.SemaphoreType.DMA((8,)),
+        ],
         compiler_params=params(),
         name="pack_cols",
-    )(meta, *([arrived] * 4))
+    )(meta, arrived)
 
 
 def place(lc):
@@ -341,7 +377,8 @@
     )(meta, own, other)
 
 
-B = 256
+B = 512
+K = 256
 H = 4
 F = 2
 ROW_STEPS = 8 // H
@@ -358,9 +395,9 @@
         for a in range(H):
             rows = slice(a * T, (a + 1) * T)
             xhi[rows, cols], xlo[rows, cols] = split(xs[d >> 1][d & 1, a])
-    for k in range(W // B):
-        n = (k + 1) * B
-        rows = slice(k * B, n)
+    for k in range(W // K):
+        n = (k + 1) * K
+        rows = slice(k * K, n)
         y_ref[:, rows] = dot3((xhi[:, :n], xlo[:, :n]), (ihi[rows, :n], ilo[rows, :n]), NT)
     at = pl.multiple_of(meta[COL_AT] * T, T)
     for a in range(H):
@@ -377,13 +414,17 @@
 def cols_step(i, inverse, x_ref, rhs, y_ref):
     ihi, ilo = inverse
     where = pl.ds(pl.multiple_of(i * B, B), B)
-    for k in range(W // B):
+    for k in range(W // K):
         x = jnp.concatenate(
-            [jnp.concatenate([x_ref[q, 0], x_ref[q, 1]], axis=1) for q in (2 * k, 2 * k + 1)], axis=0
+            [
+                jnp.concatenate([x_ref[q, n] for n in range(B // T)], axis=1)
+                for q in range(k * K // T, (k + 1) * K // T)
+            ],
+            axis=0,
         )
-        cols = slice(k * B, (k + 1) * B)
-        y = dot3((ihi[k * B :, cols], ilo[k * B :, cols]), split(x))
-        y_ref[k * B :, :] = y if k == 0 else y_ref[k * B :, :] + y
+        cols = slice(k * K, (k + 1) * K)
+        y = dot3((ihi[k * K :, cols], ilo[k * K :, cols]), split(x))
+        y_ref[k * K :, :] = y if k == 0 else y_ref[k * K :, :] + y
         rhs[0][cols, where], rhs[1][cols, where] = split(y_ref[cols, :])
 
 
@@ -430,7 +471,7 @@
 
     def col_block(i, m):
         j = part(i, ROW_STEPS, COL_STEPS)
-        return j // 4, 0, j % 4, 0, 0
+        return j // (1024 // B), 0, j % (1024 // B), 0, 0
 
     def end_block(i, m):
         return part(i, ROW_STEPS + COL_STEPS, END_STEPS), 0, 0, 0
@@ -444,7 +485,7 @@
             grid=(ROW_STEPS + COL_STEPS + END_STEPS,),
             in_specs=[whole, whole]
             + [tiles] * 4
-            + [pl.BlockSpec((None, 8, 2, T, T), col_block), pl.BlockSpec((F, 16, T, T), end_block)],
+            + [pl.BlockSpec((None, 8, B // T, T, T), col_block), pl.BlockSpec((F, 16, T, T), end_block)],
             out_specs=pl.BlockSpec((F, T, 16, T), end_block),
             scratch_shapes=[
                 pltpu.VMEM((W, W), BF16),

time: 410 us -> 403 us (0.983)
  Pallas kernels: 144 us -> 137 us
    pallas_call x2, Pallas kernels: 14.9 us -> 8.76 us  [the longest x1 4.63 us: pack_cols(): pl.pallas_call(pack_cols_kernel, in_specs=[pl.BlockSpec(memory_space=pltp...]
  transfers between devices with their start and end apart: 15 -> 15, of which waited for: 5 -> 5; matrix products, arithmetic and copies ran while one was open for 1% -> 1% of each run, Pallas kernels for 21% -> 22%
where the time goes in v4:
time: 403 us; the launch traced here: 402 us
  blocking collectives  202 us (50%)
  Pallas kernels  137 us (34%)
  starting transfers between devices  21.6 us (5%)
  waiting for transfers between devices  19.6 us (5%)
  between operations  13.6 us (3%)
  local copies, waits for them, and re-layouts  4.06 us (1%)
    all_to_all x2, blocking collectives, exchange(): return lax.all_to_all(x, axis, split_axis=0, concat_axis=0, tiled=True)  202 us
    pallas_call x1, Pallas kernels, invert(): pl.pallas_call(invert_kernel, in_specs=[pl.BlockSpec(memory_space=pltpu.S...  71.4 us
    pallas_call x1, Pallas kernels, finish(): pl.pallas_call(finish_kernel, grid_spec=pltpu.PrefetchScalarGridSpec(num_...  36.9 us
    pallas_call x2, Pallas kernels, assemble(): pl.pallas_call(functools.partial(assemble_kernel, start), grid_spec=pltpu...  16.3 us
    ppermute x4, waiting for transfers between devices, along_row(): return lax.ppermute(v, 'row', pairs)  14.6 us
    ppermute x8, starting transfers between devices, along_col(): lax.ppermute(v, 'col', [(col_id(x, y), col_id(x + dx, y + dy)) for x in r...  11.1 us
  transfers between devices with their start and end apart: 15, of which 5 were waited for; matrix products, arithmetic and copies ran while one was open for 1% of the time, Pallas kernels for 22%

profile of v4, /device:TPU:1, one launch (start us, length us, event | category | flops | bytes accessed | tf_op | source)
XLA Modules:
  0.0 402.4 jit_solution(4099946589145179451)
XLA Ops:
  6.5 0.8 reshape.8
  8.0 4.1 %pack_rows.1 = f32[16,8,128,128]{3,2,1,0:T(8,128)} custom-call(s32[130]{0:T(256)} %pad_add_fusion.meta, f32[2,4,128,8,128]{4,3,2,1,0:T(8,128)} %child.1), custom_call_target="tpu_custom_call" | custom-call | tf_op jit(solution)/shard_map/pack_rows/pallas_call | solution.py:98
  12.1 102.0 %all_to_all.10.arrived = f32[16,8,128,128]{3,2,1,0:T(8,128)} all-to-all(f32[16,8,128,128]{3,2,1,0:T(8,128)} %pack_rows.1), channel_id=1, replica_groups=mesh['row'=16,'col'=8] {'row'}, dimensions={0} | all-to-all | bytes 16777216 | tf_op jit(solution)/shard_map/all_to_all | solution.py:509
  114.1 4.6 %pack_cols.1 = f32[8,2,4,2,128,128]{5,4,3,2,1,0:T(8,128)} custom-call(s32[130]{0:T(256)} %pad_add_fusion.meta, f32[16,8,128,128]{3,2,1,0:T(8,128)} %all_to_all.10.arrived), custom_call_target="tpu_custom_call" | custom-call | tf_op jit(solution)/shard_map/pack_cols/pallas_call | solution.py:143
  118.7 100.2 %all_to_all.11.refs_0_.refs_1_.refs_2_.refs_3_.refs_4_.refs_5_.refs_6_.refs_7_ = f32[8,2,4,2,128,128]{5,4,3,2,1,0:T(8,128)} all-to-all(f32[8,2,4,2,128,128]{5,4,3,2,1,0:T(8,128)} %pack_cols.1), channel_id=1, replica_groups=mesh['row'=16,'col'=8] {'col'}, dimensions={0} | all-to-all | bytes 16777216 | tf_op jit(solution)/shard_map/all_to_all | solution.py:509
  219.0 3.8 assemble_1.1
  222.7 0.8 slice_bitcast_fusion
  223.6 2.9 collective-permute-start
  226.5 1.3 collective-permute-done
  227.8 0.8 broadcast_select_fusion
  228.6 2.8 collective-permute-start.1
  231.5 2.5 collective-permute-done.1
  234.0 1.1 slice.13
  235.1 3.1 collective-permute-start.9
  238.2 1.5 collective-permute-start.4
  239.7 0.7 collective-permute-start.3
  240.4 0.8 collective-permute-start.2
  241.2 4.0 %first_col.1 = f32[8,128,128]{2,1,0:T(8,128)} custom-call(s32[130]{0:T(256)} %pad_add_fusion.meta, f32[8,128,16,128]{3,2,1,0:T(8,128)} %front_ref.3, f32[8,2,4,2,128,128]{5,4,3,2,1,0:T(8,128)} %all_to_all.11.refs_0_.refs_1_.refs_2_.refs_3_.refs_4_.refs_5_.refs_6_.refs_7_, ...), custom_call_target="tpu_custom_call" | custom-call | tf_op jit(solution)/shard_map/first_col/pallas_call | solution.py:236
  245.2 1.2 collective-permute-done.2
  246.5 2.2 collective-permute-start.8
  248.7 2.0 collective-permute-start.7
  251.2 12.5 %assemble_8.1.m_ref = f32[8,16,128,128]{3,2,1,0:T(8,128)} custom-call(s32[130]{0:T(256)} %pad_add_fusion.meta, f32[8,128,16,128]{3,2,1,0:T(8,128)} %front_ref.3, f32[8,2,4,2,128,128]{5,4,3,2,1,0:T(8,128)} %all_to_all.11.refs_0_.refs_1_.refs_2_.refs_3_.refs_4_.refs_5_.refs_6_.refs_7_, ...), custom_call_target="tpu_custom_call" | custom-call | bytes 20971520 | tf_op jit(solution)/shard_map/assemble_8/pallas_call | solution.py:185
  263.8 0.9 slice_select_fusion
  264.8 10.8 %collective-permute-done.5 = f32[4,2,128,128]{3,2,1,0:T(8,128)} collective-permute-done((f32[4,2,128,128]{3,2,1,0:T(8,128)S(1)}, f32[4,2,128,128]{3,2,1,0:T(8,128)}, u32[]{:S(2)}, u32[]{:S(2)}) %collective-permute-start.5) | collective-permute-done | bytes 524320 | tf_op jit(solution)/shard_map/ppermute | solution.py:527
  275.7 1.4 pad_maximum_fusion.own
  277.1 2.0 collective-permute-start.10
  279.0 3.8 collective-permute-done.10.other
  282.8 1.2 collective-permute-start.13
  284.2 1.6 collective-permute-start.12
  286.0 71.4 %invert.1 = (bf16[1024,1024]{1,0:T(8,128)(2,1)}, bf16[1024,1024]{1,0:T(8,128)(2,1)}) custom-call(s32[130]{0:T(256)} %pad_add_fusion.meta, f32[4,4,2,128,128]{4,3,2,1,0:T(8,128)} %copy-done.3, f32[4,4,2,128,128]{4,3,2,1,0:T(8,128)} %copy-done.6), custom_call_target="tpu_custom_call" | custom-call | flops 80000000000 | bytes 8388608 | tf_op jit(solution)/shard_map/invert/pallas_call | solution.py:364
  357.4 0.9 copy-done.4
  358.7 36.9 %finish.1 = f32[8,128,16,128]{3,2,1,0:T(8,128)} custom-call(s32[130]{0:T(256)} %pad_add_fusion.meta, bf16[1024,1024]{1,0:T(8,128)(2,1)} %get-tuple-element.38.ihi, bf16[1024,1024]{1,0:T(8,128)(2,1)} %get-tuple-element.39.ilo, f32[2,8,128,128]{3,2,1,0:T(8,128)} %copy-done.1, f32[2,8,128,128]{3,2,1,0:T(8,128)} %collective-permute-done.11.x1, ...), custom_call_target="tpu_custom_call" | custom-call | tf_op jit(solution)/shard_map/finish/pallas_call | solution.py:481
  (32 shorter events, 2.1 us)
Async XLA Ops:
  6.5 350.9 %all-gather.3.cloned.1.call-start = ((), (), s32[]{:S(2)}) async-start(), calls=%async_computation.2 | async-start | bytes 8912896 | tf_op jit(solution)/shard_map/all_gather | solution.py:564
  223.6 4.2 %collective-permute-start = (f32[128,128]{1,0:T(8,128)S(1)}, f32[128,128]{1,0:T(8,128)S(1)}, u32[]{:S(2)}, u32[]{:S(2)}) collective-permute-start(f32[128,128]{1,0:T(8,128)S(1)} %slice_bitcast_fusion), channel_id=1, source_target_pairs={{0,64},{8,72},{16,80},{24,88},{32,96},{40,104},{48,112},{56,120},{... | collective-permute-start | bytes 196616 | tf_op jit(solution)/shard_map/ppermute | solution.py:537
  228.6 5.3 %collective-permute-start.1 = (f32[128,128]{1,0:T(8,128)S(1)}, f32[128,128]{1,0:T(8,128)S(1)}, u32[]{:S(2)}, u32[]{:S(2)}) collective-permute-start(f32[128,128]{1,0:T(8,128)S(1)} %broadcast_select_fusion), channel_id=1, source_target_pairs={{0,1},{1,0},{2,3},{3,2},{4,5},{5,4},{6,7},{7,6},{8,9},{9,8},{10,11... | collective-permute-start | bytes 196616 | tf_op jit(solution)/shard_map/ppermute | solution.py:531
  235.1 28.7 %collective-permute-start.9 = (f32[8,128,128]{2,1,0:T(8,128)S(1)}, f32[8,128,128]{2,1,0:T(8,128)S(1)}, u32[]{:S(2)}, u32[]{:S(2)}) collective-permute-start(f32[8,128,128]{2,1,0:T(8,128)S(1)} %slice.13), channel_id=1, source_target_pairs={{0,64},{8,72},{16,80},{24,88},{32,96},{40,104},{48,112},{56,120},{... | collective-permute-start | bytes 1572872 | tf_op jit(solution)/shard_map/ppermute | solution.py:537
  238.2 7.1 %collective-permute-start.4 = (f32[2,128,128]{2,1,0:T(8,128)S(1)}, f32[2,128,128]{2,1,0:T(8,128)S(1)}, u32[]{:S(2)}, u32[]{:S(2)}) collective-permute-start(f32[2,128,128]{2,1,0:T(8,128)S(1)} %pad_maximum_fusion.3), channel_id=1, source_target_pairs={{0,6},{1,7},{2,0},{3,1},{4,2},{5,3},{6,4},{7,5},{8,14},{9,15},{10,... | collective-permute-start | bytes 393224 | tf_op jit(solution)/shard_map/ppermute | solution.py:531
  239.7 5.5 %collective-permute-start.3 = (f32[2,128,128]{2,1,0:T(8,128)S(1)}, f32[2,128,128]{2,1,0:T(8,128)S(1)}, u32[]{:S(2)}, u32[]{:S(2)}) collective-permute-start(f32[2,128,128]{2,1,0:T(8,128)S(1)} %pad_maximum_fusion.3), channel_id=1, source_target_pairs={{0,4},{1,5},{2,6},{3,7},{4,0},{5,1},{6,2},{7,3},{8,12},{9,13},{10,... | collective-permute-start | bytes 393224 | tf_op jit(solution)/shard_map/ppermute | solution.py:531
  240.4 6.0 %collective-permute-start.2 = (f32[2,128,128]{2,1,0:T(8,128)S(1)}, f32[2,128,128]{2,1,0:T(8,128)S(1)}, u32[]{:S(2)}, u32[]{:S(2)}) collective-permute-start(f32[2,128,128]{2,1,0:T(8,128)S(1)} %pad_maximum_fusion.3), channel_id=1, source_target_pairs={{0,2},{1,3},{2,4},{3,5},{4,6},{5,7},{6,0},{7,1},{8,10},{9,11},{10,... | collective-permute-start | bytes 393224 | tf_op jit(solution)/shard_map/ppermute | solution.py:531
  246.4 17.3 %copy-start = (f32[1,16,128,128]{3,2,1,0:T(8,128)S(1)}, f32[1,16,128,128]{3,2,1,0:T(8,128)}, u32[]{:S(2)}) copy-start(f32[1,16,128,128]{3,2,1,0:T(8,128)} %assemble_1.1) | copy-start | bytes 3145732
  246.4 18.3 %copy-start.2 = (f32[8,128,128]{2,1,0:T(8,128)S(1)}, f32[8,128,128]{2,1,0:T(8,128)}, u32[]{:S(2)}) copy-start(f32[8,128,128]{2,1,0:T(8,128)} %first_col.1) | copy-start | bytes 1572868
  246.5 18.3 %collective-permute-start.8 = (f32[8,128,128]{2,1,0:T(8,128)}, f32[8,128,128]{2,1,0:T(8,128)S(1)}, u32[]{:S(2)}, u32[]{:S(2)}) collective-permute-start(f32[8,128,128]{2,1,0:T(8,128)} %first_col.1), channel_id=1, source_target_pairs={{0,1},{1,0},{2,3},{3,2},{4,5},{5,4},{6,7},{7,6},{8,9},{9,8},{10,11... | collective-permute-start | bytes 1572872 | tf_op jit(solution)/shard_map/ppermute | solution.py:531
  248.7 16.1 %collective-permute-start.7 = (f32[4,2,128,128]{3,2,1,0:T(8,128)S(1)}, f32[4,2,128,128]{3,2,1,0:T(8,128)S(1)}, u32[]{:S(2)}, u32[]{:S(2)}) collective-permute-start(f32[4,2,128,128]{3,2,1,0:T(8,128)S(1)} %pad_maximum_fusion.2), channel_id=1, source_target_pairs={{0,48},{8,56},{16,0},{24,8},{32,16},{40,24},{48,32},{56,40},{64,11... | collective-permute-start | bytes 1572872 | tf_op jit(solution)/shard_map/ppermute | solution.py:527
  250.6 14.2 %collective-permute-start.6 = (f32[4,2,128,128]{3,2,1,0:T(8,128)S(1)}, f32[4,2,128,128]{3,2,1,0:T(8,128)}, u32[]{:S(2)}, u32[]{:S(2)}) collective-permute-start(f32[4,2,128,128]{3,2,1,0:T(8,128)S(1)} %pad_maximum_fusion.2), channel_id=1, source_target_pairs={{0,32},{8,40},{16,48},{24,56},{32,0},{40,8},{48,16},{56,24},{64,96... | collective-permute-start | bytes 1572872 | tf_op jit(solution)/shard_map/ppermute | solution.py:527
  250.7 25.0 %collective-permute-start.5 = (f32[4,2,128,128]{3,2,1,0:T(8,128)S(1)}, f32[4,2,128,128]{3,2,1,0:T(8,128)}, u32[]{:S(2)}, u32[]{:S(2)}) collective-permute-start(f32[4,2,128,128]{3,2,1,0:T(8,128)S(1)} %pad_maximum_fusion.2), channel_id=1, source_target_pairs={{0,16},{8,24},{16,32},{24,40},{32,48},{40,56},{48,0},{56,8},{64,80... | collective-permute-start | bytes 1572872 | tf_op jit(solution)/shard_map/ppermute | solution.py:527
  264.8 20.9 %copy-start.1 = (f32[2,8,128,128]{3,2,1,0:T(8,128)}, f32[2,8,128,128]{3,2,1,0:T(8,128)S(1)}, u32[]{:S(2)}) copy-start(f32[2,8,128,128]{3,2,1,0:T(8,128)S(1)} %pad_maximum_fusion.1.x0) | copy-start | bytes 3145732
  277.0 8.9 %copy-start.3 = (f32[4,4,2,128,128]{4,3,2,1,0:T(8,128)}, f32[4,4,2,128,128]{4,3,2,1,0:T(8,128)S(1)}, u32[]{:S(2)}) copy-start(f32[4,4,2,128,128]{4,3,2,1,0:T(8,128)S(1)} %pad_maximum_fusion.own) | copy-start | bytes 6291460
  277.1 5.8 %collective-permute-start.10 = (f32[4,4,2,128,128]{4,3,2,1,0:T(8,128)S(1)}, f32[4,4,2,128,128]{4,3,2,1,0:T(8,128)S(1)}, u32[]{:S(2)}, u32[]{:S(2)}) collective-permute-start(f32[4,4,2,128,128]{4,3,2,1,0:T(8,128)S(1)} %pad_maximum_fusion.own), channel_id=1, source_target_pairs={{0,8},{8,0},{16,24},{24,16},{32,40},{40,32},{48,56},{56,48},{64,72... | collective-permute-start | bytes 6291464 | tf_op jit(solution)/shard_map/ppermute | solution.py:527
  282.8 1.3 copy-start.6
  282.8 74.6 %collective-permute-start.13 = (f32[2,8,128,128]{3,2,1,0:T(8,128)S(1)}, f32[2,8,128,128]{3,2,1,0:T(8,128)S(1)}, u32[]{:S(2)}, u32[]{:S(2)}) collective-permute-start(f32[2,8,128,128]{3,2,1,0:T(8,128)S(1)} %pad_maximum_fusion.1.x0), channel_id=1, source_target_pairs={{0,6},{1,7},{2,0},{3,1},{4,2},{5,3},{6,4},{7,5},{8,14},{9,15},{10,... | collective-permute-start | bytes 3145736 | tf_op jit(solution)/shard_map/ppermute | solution.py:531
  284.2 73.2 %collective-permute-start.12 = (f32[2,8,128,128]{3,2,1,0:T(8,128)S(1)}, f32[2,8,128,128]{3,2,1,0:T(8,128)S(1)}, u32[]{:S(2)}, u32[]{:S(2)}) collective-permute-start(f32[2,8,128,128]{3,2,1,0:T(8,128)S(1)} %pad_maximum_fusion.1.x0), channel_id=1, source_target_pairs={{0,4},{1,5},{2,6},{3,7},{4,0},{5,1},{6,2},{7,3},{8,12},{9,13},{10,... | collective-permute-start | bytes 3145736 | tf_op jit(solution)/shard_map/ppermute | solution.py:531
  285.7 71.7 %collective-permute-start.11 = (f32[2,8,128,128]{3,2,1,0:T(8,128)S(1)}, f32[2,8,128,128]{3,2,1,0:T(8,128)}, u32[]{:S(2)}, u32[]{:S(2)}) collective-permute-start(f32[2,8,128,128]{3,2,1,0:T(8,128)S(1)} %pad_maximum_fusion.1.x0), channel_id=1, source_target_pairs={{0,2},{1,3},{2,4},{3,5},{4,6},{5,7},{6,0},{7,1},{8,10},{9,11},{10,... | collective-permute-start | bytes 3145736 | tf_op jit(solution)/shard_map/ppermute | solution.py:531
  357.4 1.0 copy-start.4
  357.4 1.3 copy-start.5
Sparse Core Ops, SparseCore 0:
  275.8 49.2 all-gather.2

commit v5 on v4

--- a/solution.py
+++ b/solution.py
@@ -547,8 +547,13 @@
     landed = exchange(pack_cols(meta, arrived), "col")
     first = assemble(meta, front, landed, 0, 1)[0]
 
-    tile = jnp.where(upper, first[0], down(first[0]))
-    two = jnp.stack([tile, along_col(tile, 0, 1)])
+    tile = first[0]
+    across = [(q * 8 + c, (q + 8) * 8 + (c ^ 1)) for q in range(8) for c in range(8)]
+    two = jnp.where(
+        upper,
+        jnp.stack([tile, along_col(tile, 0, 1)]),
+        jnp.stack([down(tile), lax.ppermute(tile, ("row", "col"), across)]),
+    )
     two, first, landed, front = lax.optimization_barrier((two, first, landed, front))
     line = jnp.stack([two] + [along_col(two, dx, 0) for dx in (1, 2, 3)])
     ours = jnp.where(upper, first[:8], down(first[8:]))

time: 403 us -> 400 us (level)
    ppermute x0 -> x1, starting transfers between devices: none -> 4.58 us  [shards(): lax.ppermute(tile, ('row', 'col'), across)]
  transfers between devices with their start and end apart: 15 -> 16, of which waited for: 5 -> 4; matrix products, arithmetic and copies ran while one was open for 1% -> 1% of each run, Pallas kernels for 22% -> 22%
where the time goes in v5:
time: 400 us; the launch traced here: 399 us
  blocking collectives  202 us (50%)
  Pallas kernels  137 us (34%)
  waiting for transfers between devices  20.8 us (5%)
  starting transfers between devices  18.4 us (5%)
  between operations  13.6 us (3%)
  local copies, waits for them, and re-layouts  4.12 us (1%)
    all_to_all x2, blocking collectives, exchange(): return lax.all_to_all(x, axis, split_axis=0, concat_axis=0, tiled=True)  202 us
    pallas_call x1, Pallas kernels, invert(): pl.pallas_call(invert_kernel, in_specs=[pl.BlockSpec(memory_space=pltpu.S...  71.3 us
    pallas_call x1, Pallas kernels, finish(): pl.pallas_call(finish_kernel, grid_spec=pltpu.PrefetchScalarGridSpec(num_...  36.9 us
    pallas_call x2, Pallas kernels, assemble(): pl.pallas_call(functools.partial(assemble_kernel, start), grid_spec=pltpu...  16 us
    ppermute x4, waiting for transfers between devices, along_row(): return lax.ppermute(v, 'row', pairs)  15.8 us
  transfers between devices with their start and end apart: 16, of which 4 were waited for; matrix products, arithmetic and copies ran while one was open for 1% of the time, Pallas kernels for 22%

profile of v5, /device:TPU:1, one launch (start us, length us, event | category | flops | bytes accessed | tf_op | source)
XLA Modules:
  0.0 399.1 jit_solution(18096770654278134688)
XLA Ops:
  6.5 0.8 reshape.8
  7.3 0.6 pad_add_fusion.meta
  7.9 4.1 %pack_rows.1 = f32[16,8,128,128]{3,2,1,0:T(8,128)} custom-call(s32[130]{0:T(256)} %pad_add_fusion.meta, f32[2,4,128,8,128]{4,3,2,1,0:T(8,128)} %child.1), custom_call_target="tpu_custom_call" | custom-call | tf_op jit(solution)/shard_map/pack_rows/pallas_call | solution.py:98
  12.1 102.0 %all_to_all.10.arrived = f32[16,8,128,128]{3,2,1,0:T(8,128)} all-to-all(f32[16,8,128,128]{3,2,1,0:T(8,128)} %pack_rows.1), channel_id=1, replica_groups=mesh['row'=16,'col'=8] {'row'}, dimensions={0} | all-to-all | bytes 16777216 | tf_op jit(solution)/shard_map/all_to_all | solution.py:509
  114.1 4.6 %pack_cols.1 = f32[8,2,4,2,128,128]{5,4,3,2,1,0:T(8,128)} custom-call(s32[130]{0:T(256)} %pad_add_fusion.meta, f32[16,8,128,128]{3,2,1,0:T(8,128)} %all_to_all.10.arrived), custom_call_target="tpu_custom_call" | custom-call | tf_op jit(solution)/shard_map/pack_cols/pallas_call | solution.py:143
  118.7 100.2 %all_to_all.11.refs_0_.refs_1_.refs_2_.refs_3_.refs_4_.refs_5_.refs_6_.refs_7_ = f32[8,2,4,2,128,128]{5,4,3,2,1,0:T(8,128)} all-to-all(f32[8,2,4,2,128,128]{5,4,3,2,1,0:T(8,128)} %pack_cols.1), channel_id=1, replica_groups=mesh['row'=16,'col'=8] {'col'}, dimensions={0} | all-to-all | bytes 16777216 | tf_op jit(solution)/shard_map/all_to_all | solution.py:509
  218.9 3.6 assemble_1.1
  222.6 0.8 slice_bitcast_fusion.1
  223.4 4.6 %collective-permute-start.2 = (f32[128,128]{1,0:T(8,128)S(1)}, f32[128,128]{1,0:T(8,128)S(1)}, u32[]{:S(2)}, u32[]{:S(2)}) collective-permute-start(f32[128,128]{1,0:T(8,128)S(1)} %get-tuple-element.44), channel_id=1, source_target_pairs={{0,65},{1,64},{2,67},{3,66},{4,69},{5,68},{6,71},{7,70},{8,73},{9,... | collective-permute-start | bytes 196616 | tf_op jit(solution)/shard_map/ppermute | solution.py:555
  228.0 1.3 collective-permute-start.1
  229.3 1.3 collective-permute-start
  230.6 3.7 collective-permute-done
  234.4 1.1 slice.15
  235.4 1.3 collective-permute-start.10
  236.8 0.7 collective-permute-start.5
  237.5 1.5 collective-permute-start.4
  239.0 4.0 %first_col.1 = f32[8,128,128]{2,1,0:T(8,128)} custom-call(s32[130]{0:T(256)} %pad_add_fusion.meta, f32[8,128,16,128]{3,2,1,0:T(8,128)} %front_ref.3, f32[8,2,4,2,128,128]{5,4,3,2,1,0:T(8,128)} %all_to_all.11.refs_0_.refs_1_.refs_2_.refs_3_.refs_4_.refs_5_.refs_6_.refs_7_, ...), custom_call_target="tpu_custom_call" | custom-call | tf_op jit(solution)/shard_map/first_col/pallas_call | solution.py:236
  243.0 1.2 collective-permute-done.3
  244.2 1.2 collective-permute-start.9
  245.4 2.0 collective-permute-start.8
  247.5 0.6 collective-permute-start.6
  248.0 12.4 %assemble_8.1.m_ref = f32[8,16,128,128]{3,2,1,0:T(8,128)} custom-call(s32[130]{0:T(256)} %pad_add_fusion.meta, f32[8,128,16,128]{3,2,1,0:T(8,128)} %front_ref.3, f32[8,2,4,2,128,128]{5,4,3,2,1,0:T(8,128)} %all_to_all.11.refs_0_.refs_1_.refs_2_.refs_3_.refs_4_.refs_5_.refs_6_.refs_7_, ...), custom_call_target="tpu_custom_call" | custom-call | bytes 20971520 | tf_op jit(solution)/shard_map/assemble_8/pallas_call | solution.py:185
  260.5 0.9 slice_select_fusion
  261.5 12.0 %collective-permute-done.6 = f32[4,2,128,128]{3,2,1,0:T(8,128)} collective-permute-done((f32[4,2,128,128]{3,2,1,0:T(8,128)S(1)}, f32[4,2,128,128]{3,2,1,0:T(8,128)}, u32[]{:S(2)}, u32[]{:S(2)}) %collective-permute-start.6) | collective-permute-done | bytes 524320 | tf_op jit(solution)/shard_map/ppermute | solution.py:527
  273.5 1.4 pad_maximum_fusion.own
  274.9 0.9 collective-permute-start.11
  275.8 3.8 collective-permute-done.11.other
  279.6 1.2 collective-permute-start.14
  281.0 1.5 collective-permute-start.13
  282.8 71.3 %invert.1 = (bf16[1024,1024]{1,0:T(8,128)(2,1)}, bf16[1024,1024]{1,0:T(8,128)(2,1)}) custom-call(s32[130]{0:T(256)} %pad_add_fusion.meta, f32[4,4,2,128,128]{4,3,2,1,0:T(8,128)} %copy-done.3, f32[4,4,2,128,128]{4,3,2,1,0:T(8,128)} %copy-done.6), custom_call_target="tpu_custom_call" | custom-call | flops 80000000000 | bytes 8388608 | tf_op jit(solution)/shard_map/invert/pallas_call | solution.py:364
  354.2 0.9 copy-done.4
  355.4 36.9 %finish.1 = f32[8,128,16,128]{3,2,1,0:T(8,128)} custom-call(s32[130]{0:T(256)} %pad_add_fusion.meta, bf16[1024,1024]{1,0:T(8,128)(2,1)} %get-tuple-element.38.ihi, bf16[1024,1024]{1,0:T(8,128)(2,1)} %get-tuple-element.39.ilo, f32[2,8,128,128]{3,2,1,0:T(8,128)} %copy-done.1, f32[2,8,128,128]{3,2,1,0:T(8,128)} %collective-permute-done.12.x1, ...), custom_call_target="tpu_custom_call" | custom-call | tf_op jit(solution)/shard_map/finish/pallas_call | solution.py:481
  (33 shorter events, 1.0 us)
Async XLA Ops:
  6.5 347.6 %all-gather.3.cloned.1.call-start = ((), (), s32[]{:S(2)}) async-start(), calls=%async_computation.2 | async-start | bytes 8912896 | tf_op jit(solution)/shard_map/all_gather | solution.py:569
  223.4 7.2 %collective-permute-start.2 = (f32[128,128]{1,0:T(8,128)S(1)}, f32[128,128]{1,0:T(8,128)S(1)}, u32[]{:S(2)}, u32[]{:S(2)}) collective-permute-start(f32[128,128]{1,0:T(8,128)S(1)} %get-tuple-element.44), channel_id=1, source_target_pairs={{0,65},{1,64},{2,67},{3,66},{4,69},{5,68},{6,71},{7,70},{8,73},{9,... | collective-permute-start | bytes 196616 | tf_op jit(solution)/shard_map/ppermute | solution.py:555
  228.0 2.6 collective-permute-start.1
  229.3 5.0 %collective-permute-start = (f32[128,128]{1,0:T(8,128)S(1)}, f32[128,128]{1,0:T(8,128)S(1)}, u32[]{:S(2)}, u32[]{:S(2)}) collective-permute-start(f32[128,128]{1,0:T(8,128)S(1)} %get-tuple-element.44), channel_id=1, source_target_pairs={{0,1},{1,0},{2,3},{3,2},{4,5},{5,4},{6,7},{7,6},{8,9},{9,8},{10,11... | collective-permute-start | bytes 196616 | tf_op jit(solution)/shard_map/ppermute | solution.py:531
  235.4 25.0 %collective-permute-start.10 = (f32[8,128,128]{2,1,0:T(8,128)S(1)}, f32[8,128,128]{2,1,0:T(8,128)S(1)}, u32[]{:S(2)}, u32[]{:S(2)}) collective-permute-start(f32[8,128,128]{2,1,0:T(8,128)S(1)} %slice.15), channel_id=1, source_target_pairs={{0,64},{8,72},{16,80},{24,88},{32,96},{40,104},{48,112},{56,120},{... | collective-permute-start | bytes 1572872 | tf_op jit(solution)/shard_map/ppermute | solution.py:537
  236.8 6.2 %collective-permute-start.5 = (f32[2,128,128]{2,1,0:T(8,128)S(1)}, f32[2,128,128]{2,1,0:T(8,128)S(1)}, u32[]{:S(2)}, u32[]{:S(2)}) collective-permute-start(f32[2,128,128]{2,1,0:T(8,128)S(1)} %maximum_select_fusion), channel_id=1, source_target_pairs={{0,6},{1,7},{2,0},{3,1},{4,2},{5,3},{6,4},{7,5},{8,14},{9,15},{10,... | collective-permute-start | bytes 393224 | tf_op jit(solution)/shard_map/ppermute | solution.py:531
  237.5 5.6 %collective-permute-start.4 = (f32[2,128,128]{2,1,0:T(8,128)S(1)}, f32[2,128,128]{2,1,0:T(8,128)S(1)}, u32[]{:S(2)}, u32[]{:S(2)}) collective-permute-start(f32[2,128,128]{2,1,0:T(8,128)S(1)} %maximum_select_fusion), channel_id=1, source_target_pairs={{0,4},{1,5},{2,6},{3,7},{4,0},{5,1},{6,2},{7,3},{8,12},{9,13},{10,... | collective-permute-start | bytes 393224 | tf_op jit(solution)/shard_map/ppermute | solution.py:531
  238.9 5.2 %collective-permute-start.3 = (f32[2,128,128]{2,1,0:T(8,128)S(1)}, f32[2,128,128]{2,1,0:T(8,128)S(1)}, u32[]{:S(2)}, u32[]{:S(2)}) collective-permute-start(f32[2,128,128]{2,1,0:T(8,128)S(1)} %maximum_select_fusion), channel_id=1, source_target_pairs={{0,2},{1,3},{2,4},{3,5},{4,6},{5,7},{6,0},{7,1},{8,10},{9,11},{10,... | collective-permute-start | bytes 393224 | tf_op jit(solution)/shard_map/ppermute | solution.py:531
  244.2 16.2 %copy-start = (f32[1,16,128,128]{3,2,1,0:T(8,128)S(1)}, f32[1,16,128,128]{3,2,1,0:T(8,128)}, u32[]{:S(2)}) copy-start(f32[1,16,128,128]{3,2,1,0:T(8,128)} %assemble_1.1) | copy-start | bytes 3145732
  244.2 17.1 %copy-start.2 = (f32[8,128,128]{2,1,0:T(8,128)S(1)}, f32[8,128,128]{2,1,0:T(8,128)}, u32[]{:S(2)}) copy-start(f32[8,128,128]{2,1,0:T(8,128)} %first_col.1) | copy-start | bytes 1572868
  244.2 17.1 %collective-permute-start.9 = (f32[8,128,128]{2,1,0:T(8,128)}, f32[8,128,128]{2,1,0:T(8,128)S(1)}, u32[]{:S(2)}, u32[]{:S(2)}) collective-permute-start(f32[8,128,128]{2,1,0:T(8,128)} %first_col.1), channel_id=1, source_target_pairs={{0,1},{1,0},{2,3},{3,2},{4,5},{5,4},{6,7},{7,6},{8,9},{9,8},{10,11... | collective-permute-start | bytes 1572872 | tf_op jit(solution)/shard_map/ppermute | solution.py:531
  245.4 16.1 %collective-permute-start.8 = (f32[4,2,128,128]{3,2,1,0:T(8,128)S(1)}, f32[4,2,128,128]{3,2,1,0:T(8,128)S(1)}, u32[]{:S(2)}, u32[]{:S(2)}) collective-permute-start(f32[4,2,128,128]{3,2,1,0:T(8,128)S(1)} %pad_maximum_fusion.2), channel_id=1, source_target_pairs={{0,48},{8,56},{16,0},{24,8},{32,16},{40,24},{48,32},{56,40},{64,11... | collective-permute-start | bytes 1572872 | tf_op jit(solution)/shard_map/ppermute | solution.py:527
  247.5 14.0 %collective-permute-start.7 = (f32[4,2,128,128]{3,2,1,0:T(8,128)S(1)}, f32[4,2,128,128]{3,2,1,0:T(8,128)}, u32[]{:S(2)}, u32[]{:S(2)}) collective-permute-start(f32[4,2,128,128]{3,2,1,0:T(8,128)S(1)} %pad_maximum_fusion.2), channel_id=1, source_target_pairs={{0,32},{8,40},{16,48},{24,56},{32,0},{40,8},{48,16},{56,24},{64,96... | collective-permute-start | bytes 1572872 | tf_op jit(solution)/shard_map/ppermute | solution.py:527
  247.5 26.0 %collective-permute-start.6 = (f32[4,2,128,128]{3,2,1,0:T(8,128)S(1)}, f32[4,2,128,128]{3,2,1,0:T(8,128)}, u32[]{:S(2)}, u32[]{:S(2)}) collective-permute-start(f32[4,2,128,128]{3,2,1,0:T(8,128)S(1)} %pad_maximum_fusion.2), channel_id=1, source_target_pairs={{0,16},{8,24},{16,32},{24,40},{32,48},{40,56},{48,0},{56,8},{64,80... | collective-permute-start | bytes 1572872 | tf_op jit(solution)/shard_map/ppermute | solution.py:527
  261.5 21.0 %copy-start.1 = (f32[2,8,128,128]{3,2,1,0:T(8,128)}, f32[2,8,128,128]{3,2,1,0:T(8,128)S(1)}, u32[]{:S(2)}) copy-start(f32[2,8,128,128]{3,2,1,0:T(8,128)S(1)} %pad_maximum_fusion.1.x0) | copy-start | bytes 3145732
  274.9 7.9 %copy-start.3 = (f32[4,4,2,128,128]{4,3,2,1,0:T(8,128)}, f32[4,4,2,128,128]{4,3,2,1,0:T(8,128)S(1)}, u32[]{:S(2)}) copy-start(f32[4,4,2,128,128]{4,3,2,1,0:T(8,128)S(1)} %pad_maximum_fusion.own) | copy-start | bytes 6291460
  274.9 4.7 %collective-permute-start.11 = (f32[4,4,2,128,128]{4,3,2,1,0:T(8,128)S(1)}, f32[4,4,2,128,128]{4,3,2,1,0:T(8,128)S(1)}, u32[]{:S(2)}, u32[]{:S(2)}) collective-permute-start(f32[4,4,2,128,128]{4,3,2,1,0:T(8,128)S(1)} %pad_maximum_fusion.own), channel_id=1, source_target_pairs={{0,8},{8,0},{16,24},{24,16},{32,40},{40,32},{48,56},{56,48},{64,72... | collective-permute-start | bytes 6291464 | tf_op jit(solution)/shard_map/ppermute | solution.py:527
  279.6 1.4 copy-start.6
  279.6 74.5 %collective-permute-start.14 = (f32[2,8,128,128]{3,2,1,0:T(8,128)S(1)}, f32[2,8,128,128]{3,2,1,0:T(8,128)S(1)}, u32[]{:S(2)}, u32[]{:S(2)}) collective-permute-start(f32[2,8,128,128]{3,2,1,0:T(8,128)S(1)} %pad_maximum_fusion.1.x0), channel_id=1, source_target_pairs={{0,6},{1,7},{2,0},{3,1},{4,2},{5,3},{6,4},{7,5},{8,14},{9,15},{10,... | collective-permute-start | bytes 3145736 | tf_op jit(solution)/shard_map/ppermute | solution.py:531
  281.0 73.1 %collective-permute-start.13 = (f32[2,8,128,128]{3,2,1,0:T(8,128)S(1)}, f32[2,8,128,128]{3,2,1,0:T(8,128)S(1)}, u32[]{:S(2)}, u32[]{:S(2)}) collective-permute-start(f32[2,8,128,128]{3,2,1,0:T(8,128)S(1)} %pad_maximum_fusion.1.x0), channel_id=1, source_target_pairs={{0,4},{1,5},{2,6},{3,7},{4,0},{5,1},{6,2},{7,3},{8,12},{9,13},{10,... | collective-permute-start | bytes 3145736 | tf_op jit(solution)/shard_map/ppermute | solution.py:531
  282.5 71.6 %collective-permute-start.12 = (f32[2,8,128,128]{3,2,1,0:T(8,128)S(1)}, f32[2,8,128,128]{3,2,1,0:T(8,128)}, u32[]{:S(2)}, u32[]{:S(2)}) collective-permute-start(f32[2,8,128,128]{3,2,1,0:T(8,128)S(1)} %pad_maximum_fusion.1.x0), channel_id=1, source_target_pairs={{0,2},{1,3},{2,4},{3,5},{4,6},{5,7},{6,0},{7,1},{8,10},{9,11},{10,... | collective-permute-start | bytes 3145736 | tf_op jit(solution)/shard_map/ppermute | solution.py:531
  354.1 1.0 copy-start.4
  354.1 1.3 copy-start.5
Sparse Core Ops, SparseCore 0:
  273.6 50.1 all-gather.2
